TPU v7x, 256 devices: a whole 4x4x8 slice. The times are simulated.
256 devices in a mesh: tm: 32 (over z_lo, y, core), space: 8 (over x, z_hi).
Axes of the slice: x: 4, y: 4, z: 8 (z_hi: 2, z_lo: 4; z = z_hi * 4 + z_lo), core: 2. Of those that a mesh axis runs over, the one named last changes fastest.
Arguments:
- video_q: bfloat16 [32768, 2048], P(('tm', 'space')), may hold values from -8 to 8
- video_k: bfloat16 [32768, 2048], P(('tm', 'space')), may hold values from -8 to 8
- video_v: bfloat16 [32768, 2048], P(('tm', 'space')), may hold values from -6 to 6
- video_grad: bfloat16 [32768, 2048], P(('tm', 'space')), may hold values from -6 to 6
- audio_q: bfloat16 [16384, 2048], P('tm', 'space'), may hold values from -8 to 8
- audio_k: bfloat16 [16384, 2048], P('tm', 'space'), may hold values from -8 to 8
- audio_v: bfloat16 [16384, 2048], P('tm', 'space'), may hold values from -6 to 6
- audio_grad: bfloat16 [16384, 2048], P('tm', 'space'), may hold values from -6 to 6
- intersection_blocks: int32 [32, 2], replicated, may hold values from 0 to 1, as said below
- intersection_rows: int32 [32, 2], replicated, may hold values from 0 to 256, as said below
Outputs:
- video_out: bfloat16 [32768, 2048], P(('tm', 'space'))
- d_video_q: bfloat16 [32768, 2048], P(('tm', 'space'))
- d_video_k: bfloat16 [32768, 2048], P(('tm', 'space'))
- d_video_v: bfloat16 [32768, 2048], P(('tm', 'space'))
- audio_out: bfloat16 [16384, 2048], P('tm', 'space')
- d_audio_q: bfloat16 [16384, 2048], P('tm', 'space')
- d_audio_k: bfloat16 [16384, 2048], P('tm', 'space')
- d_audio_v: bfloat16 [16384, 2048], P('tm', 'space')
Inputs may be any that keep to these rules, and one draw needn't show every extreme that they name: `intersection_blocks`: entry [t, 0] counts an audio block of time block t - 1 and entry [t, 1] one of time block t + 1, from 0 within that time block. `intersection_rows`: entry [t, j] is 0 where that neighbouring time block does not exist (j = 0 in the first time block, j = 1 in the last).
All inputs are finite; a program needn't handle non-finite values.
Results may differ from a plain program's by a relative error of at most 0.0096.
Values may be sent and summed in bfloat16 or wider, within the bound.
A program may use at most 128 MiB of HBM per device.

v0:
```python
import jax
import jax.numpy as jnp
from jax import lax
from jax.sharding import PartitionSpec as P

HEAD_DIM = 128
BLOCK = 256
POOL = 16


def padded(block, sides, width):
    for axis, dim in sides:
        count = lax.axis_size(axis)
        forward = [(i, i + 1) for i in range(count - 1)]
        backward = [(target, source) for source, target in forward]
        low = lax.ppermute(
            lax.slice_in_dim(block, block.shape[dim] - width, None, axis=dim), axis, forward
        )
        high = lax.ppermute(lax.slice_in_dim(block, 0, width, axis=dim), axis, backward)
        block = jnp.concatenate([low, block, high], axis=dim)
    return block


def attend(queries, key_list, value_list, grad_out, allowed):
    factor = queries.shape[-1] ** (-0.5)
    offsets = jnp.where(allowed, 0.0, -jnp.inf).astype(jnp.float32)
    scores = (
        jnp.einsum("qhd,khd->hqk", queries, key_list, preferred_element_type=jnp.float32) * factor
        + offsets
    )
    row_max = jnp.max(scores, axis=2, keepdims=True)
    raised = jnp.exp(scores - row_max)
    shares = (raised / jnp.sum(raised, axis=2, keepdims=True)).astype(jnp.bfloat16)
    output_wide = jnp.einsum("hqk,khd->qhd", shares, value_list, preferred_element_type=jnp.float32)
    output = output_wide.astype(jnp.bfloat16)
    grad_values = jnp.einsum("hqk,qhd->khd", shares, grad_out, preferred_element_type=jnp.float32)
    grad_shares = jnp.einsum(
        "qhd,khd->hqk", grad_out, value_list, preferred_element_type=jnp.float32
    )
    correction = jnp.transpose(jnp.sum(grad_out.astype(jnp.float32) * output_wide, axis=2))[
        :, :, None
    ]
    grad_scores = (shares.astype(jnp.float32) * (grad_shares - correction) * factor).astype(
        jnp.bfloat16
    )
    grad_query = jnp.einsum(
        "hqk,khd->qhd", grad_scores, key_list, preferred_element_type=jnp.float32
    )
    grad_keys = jnp.einsum("hqk,qhd->khd", grad_scores, queries, preferred_element_type=jnp.float32)
    return (output, grad_query, grad_keys, grad_values)


def blocked(queries, key_list, value_list, grad_out, allowed):
    length = queries.shape[0]
    block_rows = 512
    blocks = length // block_rows
    trailing = queries.shape[1:]

    def advance(running, pieces):
        output, grad_query, grad_keys, grad_values = attend(
            pieces[0], key_list, value_list, pieces[1], allowed
        )
        return ((running[0] + grad_keys, running[1] + grad_values), (output, grad_query))

    zeroed = jnp.zeros(key_list.shape, jnp.float32)
    stacked = (
        queries.reshape((blocks, block_rows) + trailing),
        grad_out.reshape((blocks, block_rows) + trailing),
    )
    sums, outputs = lax.scan(advance, (zeroed, zeroed), stacked)
    return (outputs[0].reshape(queries.shape), outputs[1].reshape(queries.shape), sums[0], sums[1])


def take_block(stacked, first):
    return lax.dynamic_slice_in_dim(stacked, first, BLOCK, 1)


def per_device(
    video_q,
    video_k,
    video_v,
    video_grad,
    audio_q,
    audio_k,
    audio_v,
    audio_grad,
    intersection_blocks,
    intersection_rows,
):
    time_count = lax.axis_size("tm")
    time_index = lax.axis_index("tm")
    query_heads, key_heads, value_heads, grad_heads = (
        lax.all_to_all(video_q, "space", split_axis=1, concat_axis=0, tiled=True),
        lax.all_to_all(video_k, "space", split_axis=1, concat_axis=0, tiled=True),
        lax.all_to_all(video_v, "space", split_axis=1, concat_axis=0, tiled=True),
        lax.all_to_all(video_grad, "space", split_axis=1, concat_axis=0, tiled=True),
    )
    video_rows, features = query_heads.shape
    head_count = features // HEAD_DIM
    pooled_rows = video_rows // POOL
    pool_factor = POOL ** (-0.5)
    video_pair = jnp.stack([key_heads, value_heads]).reshape(2, pooled_rows, POOL, features)
    pooled = (jnp.sum(video_pair, axis=2, dtype=jnp.float32) * pool_factor).astype(jnp.bfloat16)
    near_pooled = padded(pooled, (("tm", 1),), pooled_rows)
    audio_rows = audio_q.shape[0]
    audio_pair = jnp.stack([audio_k, audio_v])
    wanted = lax.dynamic_index_in_dim(intersection_blocks, time_index, 0, keepdims=False)
    wanted_rows = lax.dynamic_index_in_dim(intersection_rows, time_index, 0, keepdims=False)
    received = padded(audio_pair, (("tm", 1),), audio_rows)
    before_block = take_block(received, wanted[0] * BLOCK)
    after_block = take_block(received, 2 * audio_rows + wanted[1] * BLOCK)
    video_keys = jnp.concatenate([key_heads, audio_k, before_block[0], after_block[0]], axis=0)
    video_values = jnp.concatenate([value_heads, audio_v, before_block[1], after_block[1]], axis=0)
    positions = jnp.arange(BLOCK, dtype=jnp.int32)
    video_allowed = jnp.concatenate(
        [
            jnp.ones((video_rows + audio_rows,), bool),
            positions < wanted_rows[0],
            positions < wanted_rows[1],
        ]
    )
    video_result = blocked(
        query_heads.reshape(video_rows, head_count, HEAD_DIM),
        video_keys.reshape(-1, head_count, HEAD_DIM),
        video_values.reshape(-1, head_count, HEAD_DIM),
        grad_heads.reshape(video_rows, head_count, HEAD_DIM),
        video_allowed,
    )
    video_output = video_result[0].reshape(video_rows, features)
    query_grads = video_result[1].reshape(video_rows, features).astype(jnp.bfloat16)
    key_terms = video_result[2].reshape(-1, features)
    value_terms = video_result[3].reshape(-1, features)
    front_back = (
        lax.all_to_all(video_output, "space", split_axis=0, concat_axis=1, tiled=True),
        lax.all_to_all(query_grads, "space", split_axis=0, concat_axis=1, tiled=True),
    )
    audio_keys = jnp.concatenate([audio_k, near_pooled[0]], axis=0)
    audio_values = jnp.concatenate([audio_v, near_pooled[1]], axis=0)
    audio_allowed = jnp.concatenate(
        [
            jnp.ones((audio_rows,), bool),
            jnp.full((pooled_rows,), time_index > 0),
            jnp.ones((pooled_rows,), bool),
            jnp.full((pooled_rows,), time_index < time_count - 1),
        ]
    )
    audio_result = blocked(
        audio_q.reshape(audio_rows, head_count, HEAD_DIM),
        audio_keys.reshape(-1, head_count, HEAD_DIM),
        audio_values.reshape(-1, head_count, HEAD_DIM),
        audio_grad.reshape(audio_rows, head_count, HEAD_DIM),
        audio_allowed,
    )
    sound_keys = audio_result[2].reshape(-1, features)
    sound_values = audio_result[3].reshape(-1, features)
    pooled_grads = jnp.stack([sound_keys[audio_rows:], sound_values[audio_rows:]])
    rim_start = video_rows + audio_rows
    own_grads = jnp.stack(
        [
            key_terms[video_rows:rim_start] + sound_keys[:audio_rows],
            value_terms[video_rows:rim_start] + sound_values[:audio_rows],
        ]
    )
    rim_before = jnp.stack(
        [key_terms[rim_start : rim_start + BLOCK], value_terms[rim_start : rim_start + BLOCK]]
    )
    rim_after = jnp.stack([key_terms[rim_start + BLOCK :], value_terms[rim_start + BLOCK :]])
    zeroed = jnp.zeros((2, audio_rows, features), jnp.float32)
    left_rims = lax.dynamic_update_slice_in_dim(zeroed, rim_before, wanted[0] * BLOCK, 1)
    right_rims = lax.dynamic_update_slice_in_dim(zeroed, rim_after, wanted[1] * BLOCK, 1)
    rim_rows = left_rims.shape[1]
    pooled_left = pooled_grads[:, :pooled_rows]
    pooled_middle = pooled_grads[:, pooled_rows : 2 * pooled_rows]
    pooled_right = pooled_grads[:, 2 * pooled_rows :]
    returned = padded(jnp.concatenate([left_rims, right_rims], axis=1), (("tm", 1),), rim_rows)
    from_earlier = returned[:, :rim_rows]
    from_later = returned[:, 3 * rim_rows :]
    pooled_back = padded(
        jnp.concatenate([pooled_left, pooled_right], axis=1), (("tm", 1),), pooled_rows
    )
    pooled_earlier = pooled_back[:, :pooled_rows]
    pooled_later = pooled_back[:, 3 * pooled_rows :]
    audio_total = own_grads + from_earlier + from_later
    pooled_total = (pooled_middle + pooled_earlier + pooled_later)[:, :, None, :] * pool_factor
    keys_back = key_terms[:video_rows].reshape(pooled_rows, POOL, features) + pooled_total[0]
    keys_back = keys_back.reshape(video_rows, features).astype(jnp.bfloat16)
    values_back = value_terms[:video_rows].reshape(pooled_rows, POOL, features) + pooled_total[1]
    values_back = values_back.reshape(video_rows, features).astype(jnp.bfloat16)
    rear_back = (
        lax.all_to_all(keys_back, "space", split_axis=0, concat_axis=1, tiled=True),
        lax.all_to_all(values_back, "space", split_axis=0, concat_axis=1, tiled=True),
    )
    video_back = (front_back[0], front_back[1], rear_back[0], rear_back[1])
    return (
        video_back[0],
        video_back[1],
        video_back[2],
        video_back[3],
        audio_result[0].reshape(audio_rows, features),
        audio_result[1].reshape(audio_rows, features).astype(jnp.bfloat16),
        audio_total[0].astype(jnp.bfloat16),
        audio_total[1].astype(jnp.bfloat16),
    )


def solution(mesh):
    return jax.shard_map(
        per_device,
        mesh=mesh,
        in_specs=(
            P(("tm", "space"), None),
            P(("tm", "space"), None),
            P(("tm", "space"), None),
            P(("tm", "space"), None),
            P("tm", "space"),
            P("tm", "space"),
            P("tm", "space"),
            P("tm", "space"),
            P(),
            P(),
        ),
        out_specs=(
            P(("tm", "space"), None),
            P(("tm", "space"), None),
            P(("tm", "space"), None),
            P(("tm", "space"), None),
            P("tm", "space"),
            P("tm", "space"),
            P("tm", "space"),
            P("tm", "space"),
        ),
        check_vma=False,
    )
```

profile of v0, /device:TPU:34, one launch (start us, length us, event | category | flops | bytes accessed | tf_op | source)
XLA Modules:
  0.0 310.0 jit_solution(2142906429610750290)
XLA Ops:
  0.7 2.1 copy.139
  2.8 10.6 %all-to-all-start.3 = ((bf16[128,8,256]{0,2,1:T(8,128)(2,1)}), bf16[128,8,256]{0,2,1:T(8,128)(2,1)S(1)}, u32[]{:S(2)}, u32[]{:S(2)}) async-start(bf16[128,8,256]{0,2,1:T(8,128)(2,1)} %bitcast.13), calls=%async_computation.3 | async-start | bytes 1048576 | tf_op jit(solution)/shard_map/all_to_all | solution.py:95
  14.4 16.1 %all-to-all-done.3 = bf16[128,8,256]{0,2,1:T(8,128)(2,1)S(1)} async-done(((bf16[128,8,256]{0,2,1:T(8,128)(2,1)}), bf16[128,8,256]{0,2,1:T(8,128)(2,1)S(1)}, u32[]{:S(2)}, u32[]{:S(2)}) %all-to-all-start.3) | async-done | bytes 524320 | tf_op jit(solution)/shard_map/all_to_all | solution.py:95
  30.5 5.9 %all-to-all-start.1 = ((bf16[128,8,256]{0,2,1:T(8,128)(2,1)}), bf16[128,8,256]{0,2,1:T(8,128)(2,1)S(1)}, u32[]{:S(2)}, u32[]{:S(2)}) async-start(bf16[128,8,256]{0,2,1:T(8,128)(2,1)} %bitcast.1), calls=%async_computation.1 | async-start | bytes 1048576 | tf_op jit(solution)/shard_map/all_to_all | solution.py:94
  37.2 12.0 %all-to-all-done.1 = bf16[128,8,256]{0,2,1:T(8,128)(2,1)S(1)} async-done(((bf16[128,8,256]{0,2,1:T(8,128)(2,1)}), bf16[128,8,256]{0,2,1:T(8,128)(2,1)S(1)}, u32[]{:S(2)}, u32[]{:S(2)}) %all-to-all-start.1) | async-done | bytes 524320 | tf_op jit(solution)/shard_map/all_to_all | solution.py:94
  50.1 6.6 %all-to-all-start = ((bf16[128,8,256]{2,0,1:T(8,128)(2,1)}), bf16[128,8,256]{2,0,1:T(8,128)(2,1)}, u32[]{:S(2)}, u32[]{:S(2)}) async-start(bf16[128,8,256]{2,0,1:T(8,128)(2,1)} %bitcast.182), calls=%async_computation | async-start | bytes 1048576 | tf_op jit(solution)/shard_map/all_to_all | solution.py:93
  57.8 1.9 collective-permute-start
  59.8 5.8 %collective-permute-start.1 = (bf16[2,512,256]{1,2,0:T(8,128)(2,1)}, bf16[2,512,256]{1,2,0:T(8,128)(2,1)}, u32[]{:S(2)}, u32[]{:S(2)}) collective-permute-start(bf16[2,512,256]{1,2,0:T(8,128)(2,1)} %pad_maximum_fusion.3), channel_id=1, source_target_pairs={{8,0},{16,8},{24,16},{32,24},{40,32},{48,40},{56,48},{64,56},{72,6... | collective-permute-start | bytes 1572872 | tf_op jit(solution)/shard_map/ppermute | solution.py:19
  74.7 9.6 %all-to-all-start.2 = ((bf16[128,8,256]{2,0,1:T(8,128)(2,1)}), bf16[128,8,256]{2,0,1:T(8,128)(2,1)}, u32[]{:S(2)}, u32[]{:S(2)}) async-start(bf16[128,8,256]{2,0,1:T(8,128)(2,1)} %bitcast.241), calls=%async_computation.2 | async-start | bytes 1048576 | tf_op jit(solution)/shard_map/all_to_all | solution.py:96
  87.6 2.0 copy.150
  94.1 1.9 collective-permute-start.2
  96.1 5.9 %collective-permute-start.3 = (bf16[2,64,256]{2,1,0:T(8,128)(2,1)}, bf16[2,64,256]{2,1,0:T(8,128)(2,1)}, u32[]{:S(2)}, u32[]{:S(2)}) collective-permute-start(bf16[2,64,256]{2,1,0:T(8,128)(2,1)} %multiply_convert_fusion.1), channel_id=1, source_target_pairs={{8,0},{16,8},{24,16},{32,24},{40,32},{48,40},{56,48},{64,56},{72,6... | collective-permute-start | bytes 196616 | tf_op jit(solution)/shard_map/ppermute | solution.py:19
  102.0 2.1 concatenate.60
  105.1 2.2 pad_maximum_fusion.1
  108.9 2.0 reshape_reshape.6
  110.8 2.0 reshape_reshape.7
  112.8 2.3 pad_maximum_fusion.2
  115.1 57.4 %while.3 = (s32[]{:T(128)}, f32[2048,2,128]{0,2,1:T(8,128)S(1)}, f32[2048,2,128]{0,2,1:T(8,128)}, bf16[2,512,2,128]{3,2,1,0:T(2,128)(2,1)}, bf16[2,512,2,128]{3,...) while((s32[]{:T(128)}, f32[2048,2,128]{0,2,1:T(8,128)S(1)}, ...), condition=%wide.region_4.5_spmd.clone, body=%wide.region_0.4_spmd.clone.sunk | while | flops 3246918656 | bytes 141069264 | solution.py:70
  115.1 2.2 constant_dynamic-slice_fusion.9
  117.3 6.7 %fusion.100 = (f32[2,512]{1,0:T(2,128)S(1)}, f32[2,512,2048]{2,1,0:T(8,128)}) fusion(f32[2048]{0:T(1024)S(1)} %broadcast_select_fusion.2, bf16[2048,2,128]{2,0,1:T(8,128)(2,1)S(1)} %get-tuple-element.347, bf16[1,512,2,128]{3,2,1,0:T(2,128)(2,1)} %get-tuple-element.311), kind=kOutput, calls=%fused_computation.98.clone.1 | convolution fusion | flops 545261568 | bytes 9711616 | tf_op jit(solution)/shard_map/while/body/eval_jaxpr/sub | solution.py:32
  123.9 4.7 %divide_convert_fusion.3 = bf16[2,512,2048]{2,1,0:T(8,128)(2,1)S(1)} fusion(f32[2,512,2048]{2,1,0:T(8,128)} %get-tuple-element.312, f32[2,512]{1,0:T(2,128)S(1)} %get-tuple-element.313), kind=kLoop, calls=%fused_computation.2.clone.1 | loop fusion | flops 4194304 | bytes 12587008 | tf_op jit(solution)/shard_map/while/body/eval_jaxpr/convert_element_type | solution.py:33
  128.7 2.0 convert_bitcast_fusion.2
  130.7 3.6 %multiply_convert_fusion.3 = bf16[2,512,2048]{2,1,0:T(8,128)(2,1)} fusion(bf16[2,512,2048]{2,1,0:T(8,128)(2,1)S(1)} %divide_convert_fusion.3, bf16[2048,2,128]{0,2,1:T(8,128)(2,1)S(1)} %copy-done.21, f32[2,512]{1,0:T(2,128)S(1)} %bitcast.263, bf16[1,512,2,128]{3,2,1,0:T(2,128)(2,1)S(1)} %copy-done.6), kind=kOutput, calls=%fused_computation.1.clone.1 | convolution fusion | flops 547356672 | bytes 9703424 | tf_op jit(solution)/shard_map/while/body/eval_jaxpr/qhd,khd->hqk/dot_general | solution.py:37
  134.3 3.6 %fusion.101 = f32[2048,2,128]{0,2,1:T(8,128)S(1)} fusion(bf16[2,512,2048]{2,1,0:T(8,128)(2,1)} %multiply_convert_fusion.3, f32[2048,2,128]{0,2,1:T(8,128)S(1)} %get-tuple-element.330, pred[]{:T(512)S(6)} %compare.3, bf16[1,512,2,128]{3,2,1,0:T(2,128)(2,1)} %get-tuple-element.311), kind=kOutput, calls=%fused_computation.11.clone.1 | convolution fusion | flops 537919488 | bytes 8650753 | tf_op jit(solution)/shard_map/while/body/eval_jaxpr/hqk,qhd->khd/dot_general | solution.py:49
  143.8 2.2 constant_dynamic-slice_fusion.9
  146.0 6.7 %fusion.100 = (f32[2,512]{1,0:T(2,128)S(1)}, f32[2,512,2048]{2,1,0:T(8,128)}) fusion(f32[2048]{0:T(1024)S(1)} %broadcast_select_fusion.2, bf16[2048,2,128]{2,0,1:T(8,128)(2,1)S(1)} %get-tuple-element.347, bf16[1,512,2,128]{3,2,1,0:T(2,128)(2,1)} %get-tuple-element.311), kind=kOutput, calls=%fused_computation.98.clone.1 | convolution fusion | flops 545261568 | bytes 9711616 | tf_op jit(solution)/shard_map/while/body/eval_jaxpr/sub | solution.py:32
  152.6 4.7 %divide_convert_fusion.3 = bf16[2,512,2048]{2,1,0:T(8,128)(2,1)S(1)} fusion(f32[2,512,2048]{2,1,0:T(8,128)} %get-tuple-element.312, f32[2,512]{1,0:T(2,128)S(1)} %get-tuple-element.313), kind=kLoop, calls=%fused_computation.2.clone.1 | loop fusion | flops 4194304 | bytes 12587008 | tf_op jit(solution)/shard_map/while/body/eval_jaxpr/convert_element_type | solution.py:33
  157.4 2.0 convert_bitcast_fusion.2
  159.4 3.6 %multiply_convert_fusion.3 = bf16[2,512,2048]{2,1,0:T(8,128)(2,1)} fusion(bf16[2,512,2048]{2,1,0:T(8,128)(2,1)S(1)} %divide_convert_fusion.3, bf16[2048,2,128]{0,2,1:T(8,128)(2,1)S(1)} %copy-done.21, f32[2,512]{1,0:T(2,128)S(1)} %bitcast.263, bf16[1,512,2,128]{3,2,1,0:T(2,128)(2,1)S(1)} %copy-done.6), kind=kOutput, calls=%fused_computation.1.clone.1 | convolution fusion | flops 547356672 | bytes 9703424 | tf_op jit(solution)/shard_map/while/body/eval_jaxpr/qhd,khd->hqk/dot_general | solution.py:37
  163.0 3.6 %fusion.101 = f32[2048,2,128]{0,2,1:T(8,128)S(1)} fusion(bf16[2,512,2048]{2,1,0:T(8,128)(2,1)} %multiply_convert_fusion.3, f32[2048,2,128]{0,2,1:T(8,128)S(1)} %get-tuple-element.330, pred[]{:T(512)S(6)} %compare.3, bf16[1,512,2,128]{3,2,1,0:T(2,128)(2,1)} %get-tuple-element.311), kind=kOutput, calls=%fused_computation.11.clone.1 | convolution fusion | flops 537919488 | bytes 8650753 | tf_op jit(solution)/shard_map/while/body/eval_jaxpr/hqk,qhd->khd/dot_general | solution.py:49
  176.6 2.4 copy.147
  179.0 2.2 convert_element_type.74
  181.1 9.6 %all-to-all-start.5 = ((bf16[8,128,256]{2,1,0:T(8,128)(2,1)}), bf16[8,128,256]{2,1,0:T(8,128)(2,1)}, u32[]{:S(2)}, u32[]{:S(2)}) async-start(bf16[8,128,256]{2,1,0:T(8,128)(2,1)} %convert_element_type.74), calls=%async_computation.5 | async-start | bytes 1048576 | tf_op jit(solution)/shard_map/all_to_all | solution.py:135
  190.7 2.2 all_to_all.110
  199.2 3.5 %fusion.57 = (f32[2,512]{1,0:T(2,128)S(1)}, f32[2,512,704]{1,2,0:T(8,128)}) fusion(f32[704]{0:T(1024)S(1)} %add_select_fusion, bf16[192,2,128]{2,0,1:T(8,128)(2,1)S(1)} %copy.153, bf16[512,2,128]{2,0,1:T(8,128)(2,1)} %copy.152, bf16[512,256]{1,0:T(8,128)(2,1)S(1)} %copy-done), kind=kOutput, calls=%fused_computation.106 | convolution fusion | flops 188154560 | bytes 3513088 | tf_op jit(solution)/shard_map/while/body/eval_jaxpr/sub | solution.py:32
  202.7 2.3 divide_convert_fusion.1
  211.4 1.9 convolution_bitcast_fusion.4
  220.1 1.9 collective-permute-start.4
  222.0 5.8 %collective-permute-start.5 = (f32[2,64,256]{2,1,0:T(8,128)}, f32[2,64,256]{2,1,0:T(8,128)}, u32[]{:S(2)}, u32[]{:S(2)}) collective-permute-start(f32[2,64,256]{2,1,0:T(8,128)} %get-tuple-element.231), channel_id=1, source_target_pairs={{8,0},{16,8},{24,16},{32,24},{40,32},{48,40},{56,48},{64,56},{72,6... | collective-permute-start | bytes 393224 | tf_op jit(solution)/shard_map/ppermute | solution.py:19
  227.8 9.6 %all-to-all-start.4 = ((bf16[8,128,256]{2,1,0:T(8,128)(2,1)}), bf16[8,128,256]{2,1,0:T(8,128)(2,1)}, u32[]{:S(2)}, u32[]{:S(2)}) async-start(bf16[8,128,256]{2,1,0:T(8,128)(2,1)} %all_to_all.110), calls=%async_computation.4 | async-start | bytes 1048576 | tf_op jit(solution)/shard_map/all_to_all | solution.py:134
  242.0 9.6 %all-to-all-done.4 = bf16[8,128,256]{2,1,0:T(8,128)(2,1)} async-done(((bf16[8,128,256]{2,1,0:T(8,128)(2,1)}), bf16[8,128,256]{2,1,0:T(8,128)(2,1)}, u32[]{:S(2)}, u32[]{:S(2)}) %all-to-all-start.4) | async-done | bytes 524320 | tf_op jit(solution)/shard_map/all_to_all | solution.py:134
  251.6 6.0 %all-to-all-start.7 = ((bf16[8,128,256]{2,1,0:T(8,128)(2,1)}), bf16[8,128,256]{2,1,0:T(8,128)(2,1)}, u32[]{:S(2)}, u32[]{:S(2)}) async-start(bf16[8,128,256]{2,1,0:T(8,128)(2,1)} %fusion.22), calls=%async_computation.7 | async-start | bytes 1048576 | tf_op jit(solution)/shard_map/all_to_all | solution.py:191
  259.5 2.9 copy.168
  264.5 1.9 collective-permute-start.6
  268.5 5.7 %collective-permute-start.7 = (f32[2,512,256]{1,2,0:T(8,128)}, f32[2,512,256]{1,2,0:T(8,128)}, u32[]{:S(2)}, u32[]{:S(2)}) collective-permute-start(f32[2,512,256]{1,2,0:T(8,128)} %maximum_dynamic-update-slice_fusion.1), channel_id=1, source_target_pairs={{8,0},{16,8},{24,16},{32,24},{40,32},{48,40},{56,48},{64,56},{72,6... | collective-permute-start | bytes 3145736 | tf_op jit(solution)/shard_map/ppermute | solution.py:19
  275.4 1.9 slice_add_fusion.1
  278.2 9.6 %all-to-all-start.6 = ((bf16[8,128,256]{2,1,0:T(8,128)(2,1)}), bf16[8,128,256]{2,1,0:T(8,128)(2,1)}, u32[]{:S(2)}, u32[]{:S(2)}) async-start(bf16[8,128,256]{2,1,0:T(8,128)(2,1)} %fusion.23), calls=%async_computation.6 | async-start | bytes 1048576 | tf_op jit(solution)/shard_map/all_to_all | solution.py:190
  287.9 2.0 slice_add_fusion
  (205 shorter events, 89.7 us)
Async XLA Ops:
  0.6 198.5 %copy-start = (bf16[512,256]{1,0:T(8,128)(2,1)S(1)}, bf16[512,256]{1,0:T(8,128)(2,1)}, u32[]{:S(2)}) copy-start(bf16[512,256]{1,0:T(8,128)(2,1)} %param.16) | copy-start | bytes 786436
  0.6 12.7 %copy-start.26 = (bf16[128,2048]{1,0:T(8,128)(2,1)S(1)}, bf16[128,2048]{1,0:T(8,128)(2,1)}, u32[]{:S(2)}) copy-start(bf16[128,2048]{1,0:T(8,128)(2,1)} %param.13) | copy-start | bytes 1572868
  0.7 35.7 %copy-start.27 = (bf16[128,2048]{1,0:T(8,128)(2,1)S(1)}, bf16[128,2048]{1,0:T(8,128)(2,1)}, u32[]{:S(2)}) copy-start(bf16[128,2048]{1,0:T(8,128)(2,1)} %param.12) | copy-start | bytes 1572868
  2.8 27.7 %all-to-all-start.3 = ((bf16[128,8,256]{0,2,1:T(8,128)(2,1)}), bf16[128,8,256]{0,2,1:T(8,128)(2,1)S(1)}, u32[]{:S(2)}, u32[]{:S(2)}) async-start(bf16[128,8,256]{0,2,1:T(8,128)(2,1)} %bitcast.13), calls=%async_computation.3 | async-start | bytes 1048576 | tf_op jit(solution)/shard_map/all_to_all | solution.py:95
  13.4 43.3 %copy-start.30 = (bf16[512,256]{1,0:T(8,128)(2,1)S(1)}, bf16[512,256]{1,0:T(8,128)(2,1)}, u32[]{:S(2)}) copy-start(bf16[512,256]{1,0:T(8,128)(2,1)} %param.17) | copy-start | bytes 786436
  14.4 42.4 %copy-start.31 = (bf16[512,256]{1,0:T(8,128)(2,1)S(1)}, bf16[512,256]{1,0:T(8,128)(2,1)}, u32[]{:S(2)}) copy-start(bf16[512,256]{1,0:T(8,128)(2,1)} %param.18) | copy-start | bytes 786436
  30.5 18.7 %all-to-all-start.1 = ((bf16[128,8,256]{0,2,1:T(8,128)(2,1)}), bf16[128,8,256]{0,2,1:T(8,128)(2,1)S(1)}, u32[]{:S(2)}, u32[]{:S(2)}) async-start(bf16[128,8,256]{0,2,1:T(8,128)(2,1)} %bitcast.1), calls=%async_computation.1 | async-start | bytes 1048576 | tf_op jit(solution)/shard_map/all_to_all | solution.py:94
  36.4 29.2 %copy-start.35 = (s32[32,2]{0,1:T(2,128)S(1)}, s32[32,2]{0,1:T(2,128)}, u32[]{:S(2)}) copy-start(s32[32,2]{0,1:T(2,128)} %param.21) | copy-start | bytes 772
  36.4 29.2 %copy-start.36 = (s32[32,2]{0,1:T(2,128)S(1)}, s32[32,2]{0,1:T(2,128)}, u32[]{:S(2)}) copy-start(s32[32,2]{0,1:T(2,128)} %param.20) | copy-start | bytes 772
  50.1 24.7 %all-to-all-start = ((bf16[128,8,256]{2,0,1:T(8,128)(2,1)}), bf16[128,8,256]{2,0,1:T(8,128)(2,1)}, u32[]{:S(2)}, u32[]{:S(2)}) async-start(bf16[128,8,256]{2,0,1:T(8,128)(2,1)} %bitcast.182), calls=%async_computation | async-start | bytes 1048576 | tf_op jit(solution)/shard_map/all_to_all | solution.py:93
  57.0 27.4 %copy-start.9 = (bf16[512,256]{0,1:T(8,128)(2,1)}, bf16[512,256]{0,1:T(8,128)(2,1)S(1)}, u32[]{:S(2)}) copy-start(bf16[512,256]{0,1:T(8,128)(2,1)S(1)} %copy.137) | copy-start | bytes 786436
  57.8 26.5 %collective-permute-start = (bf16[2,512,256]{1,2,0:T(8,128)(2,1)}, bf16[2,512,256]{1,2,0:T(8,128)(2,1)}, u32[]{:S(2)}, u32[]{:S(2)}) collective-permute-start(bf16[2,512,256]{1,2,0:T(8,128)(2,1)} %pad_maximum_fusion.3), channel_id=1, source_target_pairs={{0,8},{8,16},{16,24},{24,32},{32,40},{40,48},{48,56},{56,64},{64,7... | collective-permute-start | bytes 1572872 | tf_op jit(solution)/shard_map/ppermute | solution.py:16
  59.8 24.6 %collective-permute-start.1 = (bf16[2,512,256]{1,2,0:T(8,128)(2,1)}, bf16[2,512,256]{1,2,0:T(8,128)(2,1)}, u32[]{:S(2)}, u32[]{:S(2)}) collective-permute-start(bf16[2,512,256]{1,2,0:T(8,128)(2,1)} %pad_maximum_fusion.3), channel_id=1, source_target_pairs={{8,0},{16,8},{24,16},{32,24},{40,32},{48,40},{56,48},{64,56},{72,6... | collective-permute-start | bytes 1572872 | tf_op jit(solution)/shard_map/ppermute | solution.py:19
  74.7 36.1 %all-to-all-start.2 = ((bf16[128,8,256]{2,0,1:T(8,128)(2,1)}), bf16[128,8,256]{2,0,1:T(8,128)(2,1)}, u32[]{:S(2)}, u32[]{:S(2)}) async-start(bf16[128,8,256]{2,0,1:T(8,128)(2,1)} %bitcast.241), calls=%async_computation.2 | async-start | bytes 1048576 | tf_op jit(solution)/shard_map/all_to_all | solution.py:96
  91.8 12.3 %copy-start.19 = (bf16[8,128,256]{1,0,2:T(8,128)(2,1)S(1)}, bf16[8,128,256]{1,0,2:T(8,128)(2,1)}, u32[]{:S(2)}) copy-start(bf16[8,128,256]{1,0,2:T(8,128)(2,1)} %copy.134) | copy-start | bytes 1572868
  94.1 98.8 %collective-permute-start.2 = (bf16[2,64,256]{2,1,0:T(8,128)(2,1)}, bf16[2,64,256]{2,1,0:T(8,128)(2,1)}, u32[]{:S(2)}, u32[]{:S(2)}) collective-permute-start(bf16[2,64,256]{2,1,0:T(8,128)(2,1)} %multiply_convert_fusion.1), channel_id=1, source_target_pairs={{0,8},{8,16},{16,24},{24,32},{32,40},{40,48},{48,56},{56,64},{64,7... | collective-permute-start | bytes 196616 | tf_op jit(solution)/shard_map/ppermute | solution.py:16
  96.1 96.8 %collective-permute-start.3 = (bf16[2,64,256]{2,1,0:T(8,128)(2,1)}, bf16[2,64,256]{2,1,0:T(8,128)(2,1)}, u32[]{:S(2)}, u32[]{:S(2)}) collective-permute-start(bf16[2,64,256]{2,1,0:T(8,128)(2,1)} %multiply_convert_fusion.1), channel_id=1, source_target_pairs={{8,0},{16,8},{24,16},{32,24},{40,32},{48,40},{56,48},{64,56},{72,6... | collective-permute-start | bytes 196616 | tf_op jit(solution)/shard_map/ppermute | solution.py:19
  123.9 4.7 %copy-start.6 = (bf16[1,512,2,128]{3,2,1,0:T(2,128)(2,1)S(1)}, bf16[1,512,2,128]{3,2,1,0:T(2,128)(2,1)}, u32[]{:S(2)}) copy-start(bf16[1,512,2,128]{3,2,1,0:T(2,128)(2,1)} %get-tuple-element.314) | copy-start | bytes 786436 | tf_op jit(solution)/shard_map/while
  123.9 4.8 %copy-start.21 = (bf16[2048,2,128]{0,2,1:T(8,128)(2,1)S(1)}, bf16[2048,2,128]{0,2,1:T(8,128)(2,1)}, u32[]{:S(2)}) copy-start(bf16[2048,2,128]{0,2,1:T(8,128)(2,1)} %get-tuple-element.350) | copy-start | bytes 3145732 | tf_op jit(solution)/shard_map/while
  134.3 3.6 %copy-start.3 = (bf16[2,512,2048]{2,1,0:T(8,128)(2,1)S(1)}, bf16[2,512,2048]{2,1,0:T(8,128)(2,1)}, u32[]{:S(2)}) copy-start(bf16[2,512,2048]{2,1,0:T(8,128)(2,1)} %multiply_convert_fusion.3) | copy-start | bytes 12582916 | tf_op jit(solution)/shard_map/while
  134.3 3.6 %copy-start.28 = (bf16[2,512,2,128]{3,1,2,0:T(8,128)(2,1)S(1)}, bf16[2,512,2,128]{3,1,2,0:T(8,128)(2,1)}, u32[]{:S(2)}) copy-start(bf16[2,512,2,128]{3,1,2,0:T(8,128)(2,1)} %get-tuple-element.333) | copy-start | bytes 1572868 | tf_op jit(solution)/shard_map/while
  134.3 5.0 %copy-start.4 = (f32[2048,2,128]{0,2,1:T(8,128)S(1)}, f32[2048,2,128]{0,2,1:T(8,128)}, u32[]{:S(2)}) copy-start(f32[2048,2,128]{0,2,1:T(8,128)} %get-tuple-element.331) | copy-start | bytes 6291460 | tf_op jit(solution)/shard_map/while
  137.9 2.3 copy-start.2
  138.0 2.3 copy-start.7
  140.3 2.5 copy-start.8
  152.6 4.7 %copy-start.6 = (bf16[1,512,2,128]{3,2,1,0:T(2,128)(2,1)S(1)}, bf16[1,512,2,128]{3,2,1,0:T(2,128)(2,1)}, u32[]{:S(2)}) copy-start(bf16[1,512,2,128]{3,2,1,0:T(2,128)(2,1)} %get-tuple-element.314) | copy-start | bytes 786436 | tf_op jit(solution)/shard_map/while
  152.6 4.8 %copy-start.21 = (bf16[2048,2,128]{0,2,1:T(8,128)(2,1)S(1)}, bf16[2048,2,128]{0,2,1:T(8,128)(2,1)}, u32[]{:S(2)}) copy-start(bf16[2048,2,128]{0,2,1:T(8,128)(2,1)} %get-tuple-element.350) | copy-start | bytes 3145732 | tf_op jit(solution)/shard_map/while
  163.0 3.6 %copy-start.3 = (bf16[2,512,2048]{2,1,0:T(8,128)(2,1)S(1)}, bf16[2,512,2048]{2,1,0:T(8,128)(2,1)}, u32[]{:S(2)}) copy-start(bf16[2,512,2048]{2,1,0:T(8,128)(2,1)} %multiply_convert_fusion.3) | copy-start | bytes 12582916 | tf_op jit(solution)/shard_map/while
  163.0 3.6 %copy-start.28 = (bf16[2,512,2,128]{3,1,2,0:T(8,128)(2,1)S(1)}, bf16[2,512,2,128]{3,1,2,0:T(8,128)(2,1)}, u32[]{:S(2)}) copy-start(bf16[2,512,2,128]{3,1,2,0:T(8,128)(2,1)} %get-tuple-element.333) | copy-start | bytes 1572868 | tf_op jit(solution)/shard_map/while
  163.0 5.0 %copy-start.4 = (f32[2048,2,128]{0,2,1:T(8,128)S(1)}, f32[2048,2,128]{0,2,1:T(8,128)}, u32[]{:S(2)}) copy-start(f32[2048,2,128]{0,2,1:T(8,128)} %get-tuple-element.331) | copy-start | bytes 6291460 | tf_op jit(solution)/shard_map/while
  166.6 2.3 copy-start.2
  166.7 2.3 copy-start.7
  169.0 2.5 copy-start.8
  181.1 46.7 %all-to-all-start.5 = ((bf16[8,128,256]{2,1,0:T(8,128)(2,1)}), bf16[8,128,256]{2,1,0:T(8,128)(2,1)}, u32[]{:S(2)}, u32[]{:S(2)}) async-start(bf16[8,128,256]{2,1,0:T(8,128)(2,1)} %convert_element_type.74), calls=%async_computation.5 | async-start | bytes 1048576 | tf_op jit(solution)/shard_map/all_to_all | solution.py:135
  202.7 2.3 copy-start.32
  202.7 2.3 copy-start.34
  220.1 19.2 %collective-permute-start.4 = (f32[2,64,256]{2,1,0:T(8,128)}, f32[2,64,256]{2,1,0:T(8,128)}, u32[]{:S(2)}, u32[]{:S(2)}) collective-permute-start(f32[2,64,256]{2,1,0:T(8,128)} %get-tuple-element.230), channel_id=1, source_target_pairs={{0,8},{8,16},{16,24},{24,32},{32,40},{40,48},{48,56},{56,64},{64,7... | collective-permute-start | bytes 393224 | tf_op jit(solution)/shard_map/ppermute | solution.py:16
  222.0 17.3 %collective-permute-start.5 = (f32[2,64,256]{2,1,0:T(8,128)}, f32[2,64,256]{2,1,0:T(8,128)}, u32[]{:S(2)}, u32[]{:S(2)}) collective-permute-start(f32[2,64,256]{2,1,0:T(8,128)} %get-tuple-element.231), channel_id=1, source_target_pairs={{8,0},{16,8},{24,16},{32,24},{40,32},{48,40},{56,48},{64,56},{72,6... | collective-permute-start | bytes 393224 | tf_op jit(solution)/shard_map/ppermute | solution.py:19
  227.8 23.8 %all-to-all-start.4 = ((bf16[8,128,256]{2,1,0:T(8,128)(2,1)}), bf16[8,128,256]{2,1,0:T(8,128)(2,1)}, u32[]{:S(2)}, u32[]{:S(2)}) async-start(bf16[8,128,256]{2,1,0:T(8,128)(2,1)} %all_to_all.110), calls=%async_computation.4 | async-start | bytes 1048576 | tf_op jit(solution)/shard_map/all_to_all | solution.py:134
  251.6 26.6 %all-to-all-start.7 = ((bf16[8,128,256]{2,1,0:T(8,128)(2,1)}), bf16[8,128,256]{2,1,0:T(8,128)(2,1)}, u32[]{:S(2)}, u32[]{:S(2)}) async-start(bf16[8,128,256]{2,1,0:T(8,128)(2,1)} %fusion.22), calls=%async_computation.7 | async-start | bytes 1048576 | tf_op jit(solution)/shard_map/all_to_all | solution.py:191
  262.5 5.1 %copy-start.22 = (f32[256,2,128]{0,2,1:T(8,128)S(1)}, f32[256,2,128]{0,2,1:T(8,128)}, u32[]{:S(2)}) copy-start(f32[256,2,128]{0,2,1:T(8,128)} %get-tuple-element.221) | copy-start | bytes 786436
  264.5 37.3 %collective-permute-start.6 = (f32[2,512,256]{1,2,0:T(8,128)}, f32[2,512,256]{1,2,0:T(8,128)}, u32[]{:S(2)}, u32[]{:S(2)}) collective-permute-start(f32[2,512,256]{1,2,0:T(8,128)} %maximum_dynamic-update-slice_fusion), channel_id=1, source_target_pairs={{0,8},{8,16},{16,24},{24,32},{32,40},{40,48},{48,56},{56,64},{64,7... | collective-permute-start | bytes 3145736 | tf_op jit(solution)/shard_map/ppermute | solution.py:16
  268.5 33.3 %collective-permute-start.7 = (f32[2,512,256]{1,2,0:T(8,128)}, f32[2,512,256]{1,2,0:T(8,128)}, u32[]{:S(2)}, u32[]{:S(2)}) collective-permute-start(f32[2,512,256]{1,2,0:T(8,128)} %maximum_dynamic-update-slice_fusion.1), channel_id=1, source_target_pairs={{8,0},{16,8},{24,16},{32,24},{40,32},{48,40},{56,48},{64,56},{72,6... | collective-permute-start | bytes 3145736 | tf_op jit(solution)/shard_map/ppermute | solution.py:19
  274.5 2.8 copy-start.33
  277.3 10.5 %copy-start.16 = (f32[704,2,128]{2,0,1:T(8,128)S(1)}, f32[704,2,128]{2,0,1:T(8,128)}, u32[]{:S(2)}) copy-start(f32[704,2,128]{2,0,1:T(8,128)} %copy-done.15) | copy-start | bytes 2162692
  278.2 29.4 %all-to-all-start.6 = ((bf16[8,128,256]{2,1,0:T(8,128)(2,1)}), bf16[8,128,256]{2,1,0:T(8,128)(2,1)}, u32[]{:S(2)}, u32[]{:S(2)}) async-start(bf16[8,128,256]{2,1,0:T(8,128)(2,1)} %fusion.23), calls=%async_computation.6 | async-start | bytes 1048576 | tf_op jit(solution)/shard_map/all_to_all | solution.py:190
  287.9 4.5 %copy-start.12 = (bf16[2,512,704]{1,2,0:T(8,128)(2,1)S(1)}, bf16[2,512,704]{1,2,0:T(8,128)(2,1)}, u32[]{:S(2)}) copy-start(bf16[2,512,704]{1,2,0:T(8,128)(2,1)} %copy-done.11) | copy-start | bytes 4325380
  287.9 4.5 %copy-start.24 = (bf16[512,2,128]{2,0,1:T(8,128)(2,1)S(1)}, bf16[512,2,128]{2,0,1:T(8,128)(2,1)}, u32[]{:S(2)}) copy-start(bf16[512,2,128]{2,0,1:T(8,128)(2,1)} %copy.152) | copy-start | bytes 786436
  (16 other events, 24.0 us)
where the time goes:
time: 313 us; the launch traced here: 310 us
  starting transfers between devices  98.3 us (31%)
  local copies, waits for them, and re-layouts  92.3 us (29%)
  matrix products  45.5 us (15%)
  waiting for transfers between devices  37.8 us (12%)
  other arithmetic  33.2 us (11%)
    ppermute x4, starting transfers between devices, padded(): lax.ppermute(lax.slice_in_dim(block, 0, width, axis=dim), axis, backward)  23.2 us
    unnamed x69, local copies, waits for them, and re-layouts  22.9 us
    sub x3, matrix products, attend(): raised = jnp.exp(scores - row_max)  16.9 us
    all_to_all x1, waiting for transfers between devices, per_device(): lax.all_to_all(video_v, 'space', split_axis=1, concat_axis=0, tiled=True)  16.1 us
    all_to_all x1, waiting for transfers between devices, per_device(): lax.all_to_all(video_k, 'space', split_axis=1, concat_axis=0, tiled=True)  12 us
    convert_element_type x3, other arithmetic, attend(): (raised / jnp.sum(raised, axis=2, keepdims=True)).astype(jnp.bfloat16)  11.7 us
    all_to_all x1, starting transfers between devices, per_device(): lax.all_to_all(video_v, 'space', split_axis=1, concat_axis=0, tiled=True)  10.6 us
    all_to_all x1, starting transfers between devices, per_device(): lax.all_to_all(video_grad, 'space', split_axis=1, concat_axis=0, tiled=True)  9.63 us
  transfers between devices with their start and end apart: 16, of which 3 were waited for; matrix products, arithmetic and copies ran while one was open for 50% of the time, Pallas kernels for 0%

commit v1 on v0

v1 whole, which is shorter than its diff:
```python
import jax
import jax.numpy as jnp
from jax import lax
from jax.experimental import pallas as pl
from jax.experimental.pallas import tpu as pltpu
from jax.sharding import PartitionSpec as P

HEAD = 128
CHUNK = 256
POOL = 16
HEADS_HERE = 2
VIDEO = 1024
AUDIO = 512
POOLED = 64
OWN = VIDEO
BEFORE = VIDEO + AUDIO
AFTER = BEFORE + CHUNK
SHARED = AFTER + CHUNK
LISTED = SHARED + CHUNK
FACTOR = HEAD**-0.5
LOG2E = 1.4426950408889634
MESH = pl.DeviceIdType.MESH
F32 = jnp.float32
BF16 = jnp.bfloat16


def dot(a, b, contract=((1,), (0,))):
    return lax.dot_general(a, b, (contract, ((), ())), preferred_element_type=F32)


def kernel(
    video_q,
    video_k,
    video_v,
    video_g,
    audio_q,
    audio_k,
    audio_v,
    audio_g,
    blocks,
    rows,
    out_vo,
    out_vdq,
    out_vdk,
    out_vdv,
    out_ao,
    out_adq,
    out_adk,
    out_adv,
    keys,
    values,
    queries,
    grads,
    sound_q,
    sound_g,
    keys_t,
    values_t,
    key_sum,
    value_sum,
    scores,
    shares,
    pool_map,
    video_out,
    audio_out,
    rim_out,
    rim_grad_out,
    rim_grad_in,
    pool_grad_out,
    pool_grad_in,
    sound_sum,
    in_send,
    in_recv,
    out_send,
    out_recv,
    near_send,
    near_recv,
    local_in,
    local_sound,
    local_out,
    local_sound_out,
):
    tm = lax.axis_index("tm")
    me = lax.axis_index("space")
    x, half = lax.div(me, 2), lax.rem(me, 2)
    has_prev, has_next = tm > 0, tm < lax.axis_size("tm") - 1
    sides = ((has_prev, tm - 1), (has_next, tm + 1))

    def target(r):
        return lax.rem(x + lax.div(r, 2), 4) * 2 + lax.rem(half + lax.rem(r, 2), 2)

    def origin(r):
        return lax.rem(x + 4 - lax.div(r, 2), 4) * 2 + lax.rem(half + lax.rem(r, 2), 2)

    def rows_of(s):
        return pl.ds(pl.multiple_of(s * HEAD, HEAD), HEAD)

    def columns_of(s, j):
        return pl.ds(pl.multiple_of((s * HEADS_HERE + j) * HEAD, HEAD), HEAD)

    def head_columns(j):
        return pl.ds(pl.multiple_of(j * HEAD, HEAD), HEAD)

    sources = (video_k, video_v, video_q, video_g)
    landings = (keys, values, queries, grads)
    results = (out_vo, out_vdq, out_vdk, out_vdv)

    def in_copy(j, a, r, sender):
        s = target(r)
        slot = rows_of(me if sender else origin(r))
        index = (j * 4 + a) * 8 + r
        return pltpu.make_async_remote_copy(
            src_ref=sources[a].at[:, columns_of(s, j)],
            dst_ref=landings[a].at[j, slot, :],
            send_sem=in_send.at[index],
            recv_sem=in_recv.at[index],
            device_id=(tm, s),
            device_id_type=MESH,
        )

    def in_local(j, a):
        return pltpu.make_async_copy(
            sources[a].at[:, columns_of(me, j)],
            landings[a].at[j, rows_of(me), :],
            local_in.at[j * 4 + a],
        )

    def out_copy(j, a, r, sender):
        s = target(r)
        slot = columns_of(me if sender else origin(r), j)
        index = (j * 4 + a) * 8 + r
        return pltpu.make_async_remote_copy(
            src_ref=video_out.at[a, j, rows_of(s), :],
            dst_ref=results[a].at[:, slot],
            send_sem=out_send.at[index],
            recv_sem=out_recv.at[index],
            device_id=(tm, s),
            device_id_type=MESH,
        )

    def out_local(j, a):
        return pltpu.make_async_copy(
            video_out.at[a, j, rows_of(me), :],
            results[a].at[:, columns_of(me, j)],
            local_out.at[j * 4 + a],
        )

    sound_sources = (audio_k, audio_v, audio_q, audio_g)

    def sound_local(j, a):
        landing = (
            keys.at[j, pl.ds(OWN, AUDIO), :],
            values.at[j, pl.ds(OWN, AUDIO), :],
            sound_q.at[j],
            sound_g.at[j],
        )[a]
        return pltpu.make_async_copy(
            sound_sources[a].at[:, head_columns(j)], landing, local_sound.at[j * 4 + a]
        )

    sound_results = (out_ao, out_adq, out_adk, out_adv)

    def sound_out(j, a):
        return pltpu.make_async_copy(
            audio_out.at[a, j],
            sound_results[a].at[:, head_columns(j)],
            local_sound_out.at[j * 4 + a],
        )

    def near_copy(src, dst, index, device):
        return pltpu.make_async_remote_copy(
            src_ref=src,
            dst_ref=dst,
            send_sem=near_send.at[index],
            recv_sem=near_recv.at[index],
            device_id=(device, me),
            device_id_type=MESH,
        )

    def rim_copy(j, a, d):
        return near_copy(
            rim_out.at[d, a, j],
            (keys, values)[a].at[j, pl.ds((AFTER, BEFORE)[d], CHUNK), :],
            (j * 2 + a) * 2 + d,
            sides[d][1],
        )

    def pooled_copy(j, a, d):
        listed = (keys, values)[a]
        return near_copy(
            listed.at[j, pl.ds(SHARED + POOLED, POOLED), :],
            listed.at[j, pl.ds(SHARED + (2 * POOLED, 0)[d], POOLED), :],
            8 + (j * 2 + a) * 2 + d,
            sides[d][1],
        )

    def pool_grad_copy(j, d):
        return near_copy(
            pool_grad_out.at[d, j], pool_grad_in.at[d, j], 16 + j * 2 + d, sides[d][1]
        )

    def rim_grad_copy(j, d):
        return near_copy(
            rim_grad_out.at[d, j], rim_grad_in.at[d, j], 20 + j * 2 + d, sides[d][1]
        )

    def on_sides(act):
        for d in range(2):

            @pl.when(sides[d][0])
            def _():
                act(d)

    def from_sides(act):
        for d in range(2):

            @pl.when(sides[1 - d][0])
            def _():
                act(d)

    barrier = pltpu.get_barrier_semaphore()

    def greet(r, carry):
        pl.semaphore_signal(barrier, inc=1, device_id=(tm, target(r)), device_id_type=MESH)
        return carry

    lax.fori_loop(1, 8, greet, 0)
    on_sides(
        lambda d: pl.semaphore_signal(
            barrier, inc=1, device_id=(sides[d][1], me), device_id_type=MESH
        )
    )
    for j in range(HEADS_HERE):
        for a in range(4):
            sound_local(j, a).start()
    for j in range(HEADS_HERE):
        for a in range(4):
            in_local(j, a).start()
    pl.semaphore_wait(barrier, 7 + has_prev.astype(jnp.int32) + has_next.astype(jnp.int32))

    def send_head(j):
        for a in range(4):

            def across(i, carry, a=a):
                in_copy(j, a, 2 * i + 1, True).start()
                return carry

            def along(i, carry, a=a):
                in_copy(j, a, 2 * i, True).start()
                return carry

            lax.fori_loop(0, 4, across, 0)
            lax.fori_loop(1, 4, along, 0)

    send_head(0)

    for j in range(HEADS_HERE):
        for a in range(2):
            sound_local(j, a).wait()

    def stage_rims(d):
        weight = blocks[sides[d][1], 1 - d].astype(F32)
        for j in range(HEADS_HERE):
            for a in range(2):
                listed = (keys, values)[a]
                first = listed[j, OWN : OWN + CHUNK, :].astype(F32)
                second = listed[j, OWN + CHUNK : BEFORE, :].astype(F32)
                rim_out[d, a, j] = (first * (1.0 - weight) + second * weight).astype(BF16)
                rim_copy(j, a, d).start()

    on_sides(stage_rims)

    def fill_rims(d):
        spare = jnp.zeros((HEADS_HERE, CHUNK, HEAD), BF16)
        gone = jnp.zeros((HEADS_HERE, POOLED, HEAD), BF16)
        rim_at, pool_at = (AFTER, BEFORE)[d], SHARED + (2 * POOLED, 0)[d]
        for listed in (keys, values):
            listed[:, rim_at : rim_at + CHUNK, :] = spare
            listed[:, pool_at : pool_at + POOLED, :] = gone
        rim_grad_in[d] = jnp.zeros((HEADS_HERE, 2, CHUNK, HEAD), BF16)
        pool_grad_in[d] = jnp.zeros((HEADS_HERE, 2, POOLED, HEAD), BF16)

    for d in range(2):

        @pl.when(jnp.logical_not(sides[1 - d][0]))
        def _():
            fill_rims(d)

    for listed in (keys, values):
        listed[:, SHARED + 3 * POOLED :, :] = jnp.zeros((HEADS_HERE, POOLED, HEAD), BF16)
    group = lax.shift_right_logical(lax.broadcasted_iota(jnp.int32, (POOLED, VIDEO), 1), 4)
    member = group == lax.broadcasted_iota(jnp.int32, (POOLED, VIDEO), 0)
    pool_map[...] = jnp.where(member, 1.0, 0.0).astype(BF16)

    for a in range(4):
        lax.fori_loop(1, 8, lambda r, c, a=a: (in_copy(0, a, r, True).wait_send(), c)[1], 0)
    send_head(1)

    live = (rows[tm, 0], rows[tm, 1])
    place = lax.broadcasted_iota(jnp.int32, (CHUNK, CHUNK), 0)
    first_pooled = jnp.where(has_prev, 0, POOLED)
    last_pooled = jnp.where(has_next, 3 * POOLED, 2 * POOLED)
    video_chunks = tuple(range(8))
    audio_chunks = (4, 5, 8)

    def mask(c, s):
        if c == 6:
            return jnp.where(place < live[0], s, -jnp.inf)
        if c == 7:
            return jnp.where(place < live[1], s, -jnp.inf)
        if c == 8:
            return jnp.where((place >= first_pooled) & (place < last_pooled), s, -jnp.inf)
        return s

    def span(c):
        return slice(c * CHUNK, (c + 1) * CHUNK)

    def attend(j, chunks, q, g):
        top = None
        for i, c in enumerate(chunks):
            s = mask(c, dot(keys[j, span(c), :], q, ((1,), (1,))))
            scores[span(i), :] = s
            peak = jnp.max(s, axis=0, keepdims=True)
            top = peak if top is None else jnp.maximum(top, peak)
        total = jnp.zeros((1, CHUNK), F32)
        for i, c in enumerate(chunks):
            e = jnp.exp2((scores[span(i), :] - top) * (FACTOR * LOG2E))
            scores[span(i), :] = e
            total = total + jnp.sum(e, axis=0, keepdims=True)
        inverse = 1.0 / total
        output = jnp.zeros((HEAD, CHUNK), F32)
        for i, c in enumerate(chunks):
            p = (scores[span(i), :] * inverse).astype(BF16)
            shares[span(i), :] = p
            output = output + dot(values_t[:, span(c)], p)
            value_sum[span(c), :] += dot(p, g)
        correction = jnp.sum(g.astype(F32).T * output, axis=0, keepdims=True)
        query_grad = jnp.zeros((HEAD, CHUNK), F32)
        for i, c in enumerate(chunks):
            dp = dot(values[j, span(c), :], g, ((1,), (1,)))
            ds = (shares[span(i), :].astype(F32) * (dp - correction) * FACTOR).astype(BF16)
            query_grad = query_grad + dot(keys_t[:, span(c)], ds)
            key_sum[span(c), :] += dot(ds, q)
        return output.T.astype(BF16), query_grad.T.astype(BF16)

    def head(j, carry):
        for a in range(2):
            in_local(j, a).wait()
            lax.fori_loop(1, 8, lambda r, c, a=a: (in_copy(j, a, r, False).wait_recv(), c)[1], 0)
        for a, listed in enumerate((keys, values)):
            pooled = dot(pool_map[...], listed[j, :VIDEO, :]) * (POOL**-0.5)
            listed[j, SHARED + POOLED : SHARED + 2 * POOLED, :] = pooled.astype(BF16)
            on_sides(lambda d, a=a: pooled_copy(j, a, d).start())
        for a in range(2):
            from_sides(lambda d, a=a: rim_copy(j, a, d).wait_recv())
        for c in range(8):
            keys_t[:, span(c)] = keys[j, span(c), :].astype(F32).T.astype(BF16)
            values_t[:, span(c)] = values[j, span(c), :].astype(F32).T.astype(BF16)
        key_sum[...] = jnp.zeros_like(key_sum)
        value_sum[...] = jnp.zeros_like(value_sum)
        for a in range(2):
            from_sides(lambda d, a=a: pooled_copy(j, a, d).wait_recv())
        keys_t[:, span(8)] = keys[j, span(8), :].astype(F32).T.astype(BF16)
        values_t[:, span(8)] = values[j, span(8), :].astype(F32).T.astype(BF16)
        for a in (2, 3):
            sound_local(j, a).wait()

        def sound_step(i, c):
            part = pl.ds(pl.multiple_of(i * CHUNK, CHUNK), CHUNK)
            o, dq = attend(j, audio_chunks, sound_q[j, part, :], sound_g[j, part, :])
            audio_out[0, j, part, :] = o
            audio_out[1, j, part, :] = dq
            return c

        lax.fori_loop(0, AUDIO // CHUNK, sound_step, 0)
        sound_out(j, 0).start()
        sound_out(j, 1).start()
        for d in range(2):
            at = SHARED + (0, 2 * POOLED)[d]
            pool_grad_out[d, j, 0] = key_sum[at : at + POOLED, :].astype(BF16)
            pool_grad_out[d, j, 1] = value_sum[at : at + POOLED, :].astype(BF16)
        on_sides(lambda d: pool_grad_copy(j, d).start())

        for a in (2, 3):
            in_local(j, a).wait()
            lax.fori_loop(1, 8, lambda r, c, a=a: (in_copy(j, a, r, False).wait_recv(), c)[1], 0)

        def video_step(k, c):
            i = lax.rem(x + k, 4)
            part = pl.ds(pl.multiple_of(i * CHUNK, CHUNK), CHUNK)
            o, dq = attend(j, video_chunks, queries[j, part, :], grads[j, part, :])
            video_out[0, j, part, :] = o
            video_out[1, j, part, :] = dq
            for a in range(2):
                out_copy(j, a, 2 * k + 1, True).start()

                @pl.when(k == 0)
                def _(a=a):
                    out_local(j, a).start()

                @pl.when(k > 0)
                def _(a=a):
                    out_copy(j, a, 2 * k, True).start()

            return c

        lax.fori_loop(0, 4, video_step, 0)
        for d in range(2):
            at = (BEFORE, AFTER)[d]
            rim_grad_out[d, j, 0] = key_sum[at : at + CHUNK, :].astype(BF16)
            rim_grad_out[d, j, 1] = value_sum[at : at + CHUNK, :].astype(BF16)
        on_sides(lambda d: rim_grad_copy(j, d).start())
        from_sides(lambda d: pool_grad_copy(j, d).wait_recv())
        for a, summed in enumerate((key_sum, value_sum)):
            pooled = summed[SHARED + POOLED : SHARED + 2 * POOLED, :]
            for d in range(2):
                pooled = pooled + pool_grad_in[d, j, a].astype(F32)
            pooled = pooled * (POOL**-0.5)
            spread = jnp.broadcast_to(pooled[:, None, :], (POOLED, POOL, HEAD))
            whole = summed[:VIDEO, :] + spread.reshape(VIDEO, HEAD)
            video_out[2 + a, j] = whole.astype(BF16)
            out_local(j, 2 + a).start()

            def across(i, c, a=a):
                out_copy(j, 2 + a, 2 * i + 1, True).start()
                return c

            def along(i, c, a=a):
                out_copy(j, 2 + a, 2 * i, True).start()
                return c

            lax.fori_loop(0, 4, across, 0)
            lax.fori_loop(1, 4, along, 0)
            sound_sum[j, a] = summed[OWN:BEFORE, :]
        return carry

    lax.fori_loop(0, HEADS_HERE, head, 0)

    prev_weight = blocks[jnp.maximum(tm - 1, 0), 1].astype(F32)
    next_weight = blocks[jnp.minimum(tm + 1, lax.axis_size("tm") - 1), 0].astype(F32)
    weights = (next_weight, prev_weight)
    for j in range(HEADS_HERE):
        from_sides(lambda d, j=j: rim_grad_copy(j, d).wait_recv())
        for a in range(2):
            for b in range(2):
                part = slice(b * CHUNK, (b + 1) * CHUNK)
                whole = sound_sum[j, a, part, :]
                for d in range(2):
                    weight = weights[d] if b else 1.0 - weights[d]
                    whole = whole + rim_grad_in[d, j, a].astype(F32) * weight
                audio_out[2 + a, j, part, :] = whole.astype(BF16)
            sound_out(j, 2 + a).start()

    for j in range(HEADS_HERE):
        for a in range(4):
            sound_out(j, a).wait()
            out_local(j, a).wait()
            lax.fori_loop(1, 8, lambda r, c, j=j, a=a: (out_copy(j, a, r, True).wait_send(), c)[1], 0)
            lax.fori_loop(1, 8, lambda r, c, j=j, a=a: (out_copy(j, a, r, False).wait_recv(), c)[1], 0)
        for a in range(2):
            on_sides(lambda d, j=j, a=a: rim_copy(j, a, d).wait_send())
            on_sides(lambda d, j=j, a=a: pooled_copy(j, a, d).wait_send())
        on_sides(lambda d, j=j: pool_grad_copy(j, d).wait_send())
        on_sides(lambda d, j=j: rim_grad_copy(j, d).wait_send())
    for a in range(4):
        lax.fori_loop(1, 8, lambda r, c, a=a: (in_copy(1, a, r, True).wait_send(), c)[1], 0)


def per_device(*args):
    video = jax.ShapeDtypeStruct(args[0].shape, BF16)
    audio = jax.ShapeDtypeStruct(args[4].shape, BF16)
    two = HEADS_HERE
    return pl.pallas_call(
        kernel,
        out_shape=(video,) * 4 + (audio,) * 4,
        in_specs=[pl.BlockSpec(memory_space=pl.ANY)] * 8
        + [pl.BlockSpec(memory_space=pltpu.SMEM)] * 2,
        out_specs=(pl.BlockSpec(memory_space=pl.ANY),) * 8,
        scratch_shapes=[
            pltpu.VMEM((two, LISTED, HEAD), BF16),
            pltpu.VMEM((two, LISTED, HEAD), BF16),
            pltpu.VMEM((two, VIDEO, HEAD), BF16),
            pltpu.VMEM((two, VIDEO, HEAD), BF16),
            pltpu.VMEM((two, AUDIO, HEAD), BF16),
            pltpu.VMEM((two, AUDIO, HEAD), BF16),
            pltpu.VMEM((HEAD, LISTED), BF16),
            pltpu.VMEM((HEAD, LISTED), BF16),
            pltpu.VMEM((LISTED, HEAD), F32),
            pltpu.VMEM((LISTED, HEAD), F32),
            pltpu.VMEM((SHARED, CHUNK), F32),
            pltpu.VMEM((SHARED, CHUNK), BF16),
            pltpu.VMEM((POOLED, VIDEO), BF16),
            pltpu.VMEM((4, two, VIDEO, HEAD), BF16),
            pltpu.VMEM((4, two, AUDIO, HEAD), BF16),
            pltpu.VMEM((2, 2, two, CHUNK, HEAD), BF16),
            pltpu.VMEM((2, two, 2, CHUNK, HEAD), BF16),
            pltpu.VMEM((2, two, 2, CHUNK, HEAD), BF16),
            pltpu.VMEM((2, two, 2, POOLED, HEAD), BF16),
            pltpu.VMEM((2, two, 2, POOLED, HEAD), BF16),
            pltpu.VMEM((two, 2, AUDIO, HEAD), F32),
            pltpu.SemaphoreType.DMA((64,)),
            pltpu.SemaphoreType.DMA((64,)),
            pltpu.SemaphoreType.DMA((64,)),
            pltpu.SemaphoreType.DMA((64,)),
            pltpu.SemaphoreType.DMA((24,)),
            pltpu.SemaphoreType.DMA((24,)),
            pltpu.SemaphoreType.DMA((8,)),
            pltpu.SemaphoreType.DMA((8,)),
            pltpu.SemaphoreType.DMA((8,)),
            pltpu.SemaphoreType.DMA((8,)),
        ],
        compiler_params=pltpu.CompilerParams(
            collective_id=0, has_side_effects=True, vmem_limit_bytes=48 * 1024 * 1024
        ),
        name="joint_attention",
    )(*args)


def solution(mesh):
    tokens, sound = P(("tm", "space"), None), P("tm", "space")
    return jax.shard_map(
        per_device,
        mesh=mesh,
        in_specs=(tokens,) * 4 + (sound,) * 4 + (P(), P()),
        out_specs=(tokens,) * 4 + (sound,) * 4,
        check_vma=False,
    )
```

time: 313 us -> 140 us (0.45)
  Pallas kernels: 0 us -> 124 us
  starting transfers between devices: 98.3 us -> 0 us
  local copies, waits for them, and re-layouts: 92.3 us -> 13.8 us
  matrix products: 45.5 us -> 0 us
  waiting for transfers between devices: 37.8 us -> 0 us
  other arithmetic: 33.2 us -> 0 us
    pallas_call x0 -> x1, Pallas kernels: none -> 124 us  [per_device(): pl.pallas_call(kernel, out_shape=(video,) * 4 + (audio,) * 4, in_specs=[p...]
    all_to_all x8 -> x0, starting transfers between devices: 67.5 us -> none  [the longest x1 10.6 us: per_device(): lax.all_to_all(video_v, 'space', split_axis=1, concat_axis=0, tiled=True)]
    all_to_all x8 -> x0, waiting for transfers between devices: 37.8 us -> none  [the longest x1 16.1 us: per_device(): lax.all_to_all(video_v, 'space', split_axis=1, concat_axis=0, tiled=True)]
    ppermute x8 -> x0, starting transfers between devices: 30.8 us -> none  [the longest x4 23.2 us: padded(): lax.ppermute(lax.slice_in_dim(block, 0, width, axis=dim), axis, backward)]
    dot_general x15 -> x0, matrix products: 28.7 us -> none  [the longest x3 7.77 us: attend(): jnp.einsum('qhd,khd->hqk', grad_out, value_list, preferred_element_type=j...]
    sub x3 -> x0, matrix products: 16.9 us -> none  [attend(): raised = jnp.exp(scores - row_max)]
    all_to_all x11 -> x0, local copies, waits for them, and re-layouts: 15.4 us -> none  [the longest x2 3.48 us: per_device(): lax.all_to_all(video_output, 'space', split_axis=0, concat_axis=1, tiled=...]
    convert_element_type x6 -> x0, other arithmetic: 14.2 us -> none  [the longest x3 11.7 us: attend(): (raised / jnp.sum(raised, axis=2, keepdims=True)).astype(jnp.bfloat16)]
  transfers between devices with their start and end apart: 16 -> 0, of which waited for: 3 -> 0; matrix products, arithmetic and copies ran while one was open for 50% -> 0% of each run, Pallas kernels for 0% -> 0%
where the time goes in v1:
time: 140 us; the launch traced here: 138 us
  Pallas kernels  124 us (89%)
  local copies, waits for them, and re-layouts  13.8 us (10%)
    pallas_call x1, Pallas kernels, per_device(): pl.pallas_call(kernel, out_shape=(video,) * 4 + (audio,) * 4, in_specs=[p...  124 us
    unnamed x26, local copies, waits for them, and re-layouts  13.8 us

profile of v1, /device:TPU:34, one launch (start us, length us, event | category | flops | bytes accessed | tf_op | source)
XLA Modules:
  0.0 138.2 jit_solution(984712506149281875)
XLA Ops:
  0.6 0.0 copy-start.7
  0.6 0.8 copy.18.blocks
  1.4 0.0 copy-done.7
  1.4 0.1 copy.19.rows
  1.5 0.0 copy-start
  1.5 1.0 copy-done
  2.5 0.0 copy-start.1
  2.5 1.0 copy-done.1
  3.6 0.0 copy-start.2
  3.6 1.0 copy-done.2
  4.6 0.0 copy-start.3
  4.6 0.9 copy-done.3
  5.6 0.0 copy-start.4
  5.6 0.9 copy-done.4
  6.5 0.0 copy-start.5
  6.5 0.9 copy-done.5
  7.5 0.0 copy-start.6
  7.5 0.9 copy-done.6
  8.4 123.8 %joint_attention.1 = (bf16[128,2048]{1,0:T(8,128)(2,1)S(1)}, bf16[128,2048]{1,0:T(8,128)(2,1)S(1)}, bf16[128,2048]{1,0:T(8,128)(2,1)S(1)}, bf16[128,2048]{1,0:T(...) custom-call(bf16[128,2048]{1,0:T(8,128)(2,1)S(1)} %copy-done, ...), custom_call_target="tpu_custom_call" | custom-call | tf_op jit(solution)/shard_map/joint_attention/pallas_call | solution.py:472
  132.2 0.8 copy.28
  133.0 0.8 copy.29
  133.8 0.8 copy.30
  134.6 0.8 copy.31
  135.4 0.7 copy.32
  136.1 0.7 copy.33
  136.8 0.7 copy.34
  137.5 0.7 copy.35
Async XLA Ops:
  0.6 0.8 copy-start.7
  1.5 1.0 copy-start
  2.5 1.0 copy-start.1
  3.6 1.0 copy-start.2
  4.6 0.9 copy-start.3
  5.6 0.9 copy-start.4
  6.5 0.9 copy-start.5
  7.5 0.9 copy-start.6

commit v2 on v1

--- a/solution.py
+++ b/solution.py
@@ -59,7 +59,10 @@
     value_sum,
     scores,
     shares,
-    pool_map,
+    rows_k,
+    rows_v,
+    pool_stage,
+    pool_land,
     video_out,
     audio_out,
     rim_out,
@@ -67,13 +70,15 @@
     rim_grad_in,
     pool_grad_out,
     pool_grad_in,
-    sound_sum,
     in_send,
     in_recv,
     out_send,
     out_recv,
     near_send,
     near_recv,
+    pool_send,
+    pool_recv,
+    local_rows,
     local_in,
     local_sound,
     local_out,
@@ -117,6 +122,20 @@
             device_id_type=MESH,
         )
 
+    def pool_copy(r):
+        s = target(r)
+        return pltpu.make_async_remote_copy(
+            src_ref=pool_stage.at[s],
+            dst_ref=pool_land.at[me],
+            send_sem=pool_send.at[r],
+            recv_sem=pool_recv.at[r],
+            device_id=(tm, s),
+            device_id_type=MESH,
+        )
+
+    def rows_local(a):
+        return pltpu.make_async_copy(sources[a], (rows_k, rows_v)[a], local_rows.at[a])
+
     def in_local(j, a):
         return pltpu.make_async_copy(
             sources[a].at[:, columns_of(me, j)],
@@ -198,9 +217,13 @@
             pool_grad_out.at[d, j], pool_grad_in.at[d, j], 16 + j * 2 + d, sides[d][1]
         )
 
-    def rim_grad_copy(j, d):
+    def rim_grad_copy(j, d, i):
+        a, part = i // 4, pl.ds(i % 4 * POOLED, POOLED)
         return near_copy(
-            rim_grad_out.at[d, j], rim_grad_in.at[d, j], 20 + j * 2 + d, sides[d][1]
+            rim_grad_out.at[d, j, a, part, :],
+            rim_grad_in.at[d, j, a, part, :],
+            20 + (j * 2 + d) * 8 + i,
+            sides[d][1],
         )
 
     def on_sides(act):
@@ -229,43 +252,27 @@
             barrier, inc=1, device_id=(sides[d][1], me), device_id_type=MESH
         )
     )
+    for a in range(2):
+        rows_local(a).start()
     for j in range(HEADS_HERE):
         for a in range(4):
             sound_local(j, a).start()
     for j in range(HEADS_HERE):
         for a in range(4):
             in_local(j, a).start()
-    pl.semaphore_wait(barrier, 7 + has_prev.astype(jnp.int32) + has_next.astype(jnp.int32))
-
-    def send_head(j):
-        for a in range(4):
-
-            def across(i, carry, a=a):
-                in_copy(j, a, 2 * i + 1, True).start()
-                return carry
-
-            def along(i, carry, a=a):
-                in_copy(j, a, 2 * i, True).start()
-                return carry
-
-            lax.fori_loop(0, 4, across, 0)
-            lax.fori_loop(1, 4, along, 0)
-
-    send_head(0)
 
     for j in range(HEADS_HERE):
         for a in range(2):
             sound_local(j, a).wait()
 
     def stage_rims(d):
-        weight = blocks[sides[d][1], 1 - d].astype(F32)
+        weight = blocks[1 - d, sides[d][1]].astype(F32)
         for j in range(HEADS_HERE):
             for a in range(2):
                 listed = (keys, values)[a]
                 first = listed[j, OWN : OWN + CHUNK, :].astype(F32)
                 second = listed[j, OWN + CHUNK : BEFORE, :].astype(F32)
                 rim_out[d, a, j] = (first * (1.0 - weight) + second * weight).astype(BF16)
-                rim_copy(j, a, d).start()
 
     on_sides(stage_rims)
 
@@ -287,15 +294,60 @@
 
     for listed in (keys, values):
         listed[:, SHARED + 3 * POOLED :, :] = jnp.zeros((HEADS_HERE, POOLED, HEAD), BF16)
-    group = lax.shift_right_logical(lax.broadcasted_iota(jnp.int32, (POOLED, VIDEO), 1), 4)
-    member = group == lax.broadcasted_iota(jnp.int32, (POOLED, VIDEO), 0)
-    pool_map[...] = jnp.where(member, 1.0, 0.0).astype(BF16)
-
-    for a in range(4):
-        lax.fori_loop(1, 8, lambda r, c, a=a: (in_copy(0, a, r, True).wait_send(), c)[1], 0)
-    send_head(1)
-
-    live = (rows[tm, 0], rows[tm, 1])
+    member = lax.broadcasted_iota(jnp.int32, (POOL, HEAD), 0)
+    group = lax.shift_right_logical(lax.broadcasted_iota(jnp.int32, (POOL, HEAD), 1), 4)
+    upper = jnp.where(member == group, 1.0, 0.0).astype(BF16)
+    lower = jnp.where(member == group + 8, 1.0, 0.0).astype(BF16)
+    for a in range(2):
+        rows_local(a).wait()
+    for s in range(8):
+        for j in range(HEADS_HERE):
+            part = slice((s * HEADS_HERE + j) * HEAD, (s * HEADS_HERE + j + 1) * HEAD)
+            both = dot(upper, rows_k[:, part]) + dot(lower, rows_v[:, part])
+            pool_stage[s, j] = (both * (POOL**-0.5)).astype(BF16)
+
+    pl.semaphore_wait(barrier, 7 + has_prev.astype(jnp.int32) + has_next.astype(jnp.int32))
+
+    def to_peers(act):
+        lax.fori_loop(0, 4, lambda i, c: (act(2 * i + 1), c)[1], 0)
+        lax.fori_loop(1, 4, lambda i, c: (act(2 * i), c)[1], 0)
+
+    def send_in(j, a):
+        to_peers(lambda r: in_copy(j, a, r, True).start())
+
+    def sent_in(j, a):
+        to_peers(lambda r: in_copy(j, a, r, True).wait_send())
+
+    def came_in(j, a):
+        in_local(j, a).wait()
+        to_peers(lambda r: in_copy(j, a, r, False).wait_recv())
+
+    def send_out(j, a):
+        out_local(j, a).start()
+        to_peers(lambda r: out_copy(j, a, r, True).start())
+
+    def send_rims(j):
+        for a in range(2):
+            on_sides(lambda d, a=a: rim_copy(j, a, d).start())
+
+    to_peers(lambda r: pool_copy(r).start())
+    send_in(0, 0)
+    send_in(0, 1)
+    send_rims(0)
+    pool_land[me] = pool_stage[me]
+    to_peers(lambda r: pool_copy(r).wait_recv())
+    for j in range(HEADS_HERE):
+        landed = [pool_land[s, j].astype(F32) for s in range(8)]
+        for a, listed in enumerate((keys, values)):
+            pooled = jnp.concatenate([t[a * 8 : a * 8 + 8] for t in landed], axis=0)
+            listed[j, SHARED + POOLED : SHARED + 2 * POOLED, :] = pooled.astype(BF16)
+            on_sides(lambda d, j=j, a=a: pooled_copy(j, a, d).start())
+    send_in(0, 2)
+    send_in(0, 3)
+    key_sum[...] = jnp.zeros_like(key_sum)
+    value_sum[...] = jnp.zeros_like(value_sum)
+
+    live = (rows[0, tm], rows[1, tm])
     place = lax.broadcasted_iota(jnp.int32, (CHUNK, CHUNK), 0)
     first_pooled = jnp.where(has_prev, 0, POOLED)
     last_pooled = jnp.where(has_next, 3 * POOLED, 2 * POOLED)
@@ -331,119 +383,111 @@
         for i, c in enumerate(chunks):
             p = (scores[span(i), :] * inverse).astype(BF16)
             shares[span(i), :] = p
-            output = output + dot(values_t[:, span(c)], p)
-            value_sum[span(c), :] += dot(p, g)
+            output = output + dot(values_t[j, :, span(c)], p)
+            value_sum[j, span(c), :] += dot(p, g)
         correction = jnp.sum(g.astype(F32).T * output, axis=0, keepdims=True)
         query_grad = jnp.zeros((HEAD, CHUNK), F32)
         for i, c in enumerate(chunks):
             dp = dot(values[j, span(c), :], g, ((1,), (1,)))
             ds = (shares[span(i), :].astype(F32) * (dp - correction) * FACTOR).astype(BF16)
-            query_grad = query_grad + dot(keys_t[:, span(c)], ds)
-            key_sum[span(c), :] += dot(ds, q)
+            query_grad = query_grad + dot(keys_t[j, :, span(c)], ds)
+            key_sum[j, span(c), :] += dot(ds, q)
         return output.T.astype(BF16), query_grad.T.astype(BF16)
 
-    def head(j, carry):
-        for a in range(2):
-            in_local(j, a).wait()
-            lax.fori_loop(1, 8, lambda r, c, a=a: (in_copy(j, a, r, False).wait_recv(), c)[1], 0)
-        for a, listed in enumerate((keys, values)):
-            pooled = dot(pool_map[...], listed[j, :VIDEO, :]) * (POOL**-0.5)
-            listed[j, SHARED + POOLED : SHARED + 2 * POOLED, :] = pooled.astype(BF16)
-            on_sides(lambda d, a=a: pooled_copy(j, a, d).start())
-        for a in range(2):
-            from_sides(lambda d, a=a: rim_copy(j, a, d).wait_recv())
-        for c in range(8):
-            keys_t[:, span(c)] = keys[j, span(c), :].astype(F32).T.astype(BF16)
-            values_t[:, span(c)] = values[j, span(c), :].astype(F32).T.astype(BF16)
-        key_sum[...] = jnp.zeros_like(key_sum)
-        value_sum[...] = jnp.zeros_like(value_sum)
+    def finish(j):
+        from_sides(lambda d: pool_grad_copy(j, d).wait_recv())
+        for a, summed in enumerate((key_sum, value_sum)):
+            pooled = summed[j, SHARED + POOLED : SHARED + 2 * POOLED, :]
+            for d in range(2):
+                pooled = pooled + pool_grad_in[d, j, a].astype(F32)
+            pooled = pooled * (POOL**-0.5)
+            spread = jnp.broadcast_to(pooled[:, None, :], (POOLED, POOL, HEAD))
+            whole = summed[j, :VIDEO, :] + spread.reshape(VIDEO, HEAD)
+            video_out[2 + a, j] = whole.astype(BF16)
+            send_out(j, 2 + a)
+
+    def turn(j, c):
+        keys_t[j, :, span(c)] = keys[j, span(c), :].astype(F32).T.astype(BF16)
+        values_t[j, :, span(c)] = values[j, span(c), :].astype(F32).T.astype(BF16)
+
+    def sound(j, carry):
+        turn(j, 4)
+        turn(j, 5)
+        for a in (2, 3):
+            sound_local(j, a).wait()
         for a in range(2):
             from_sides(lambda d, a=a: pooled_copy(j, a, d).wait_recv())
-        keys_t[:, span(8)] = keys[j, span(8), :].astype(F32).T.astype(BF16)
-        values_t[:, span(8)] = values[j, span(8), :].astype(F32).T.astype(BF16)
-        for a in (2, 3):
-            sound_local(j, a).wait()
-
-        def sound_step(i, c):
+        turn(j, 8)
+
+        def step(i, c):
             part = pl.ds(pl.multiple_of(i * CHUNK, CHUNK), CHUNK)
             o, dq = attend(j, audio_chunks, sound_q[j, part, :], sound_g[j, part, :])
             audio_out[0, j, part, :] = o
             audio_out[1, j, part, :] = dq
             return c
 
-        lax.fori_loop(0, AUDIO // CHUNK, sound_step, 0)
+        lax.fori_loop(0, AUDIO // CHUNK, step, 0)
+        for d in range(2):
+            at = SHARED + (0, 2 * POOLED)[d]
+            pool_grad_out[d, j, 0] = key_sum[j, at : at + POOLED, :].astype(BF16)
+            pool_grad_out[d, j, 1] = value_sum[j, at : at + POOLED, :].astype(BF16)
+        on_sides(lambda d: pool_grad_copy(j, d).start())
         sound_out(j, 0).start()
         sound_out(j, 1).start()
-        for d in range(2):
-            at = SHARED + (0, 2 * POOLED)[d]
-            pool_grad_out[d, j, 0] = key_sum[at : at + POOLED, :].astype(BF16)
-            pool_grad_out[d, j, 1] = value_sum[at : at + POOLED, :].astype(BF16)
-        on_sides(lambda d: pool_grad_copy(j, d).start())
-
-        for a in (2, 3):
-            in_local(j, a).wait()
-            lax.fori_loop(1, 8, lambda r, c, a=a: (in_copy(j, a, r, False).wait_recv(), c)[1], 0)
-
-        def video_step(k, c):
+
+        @pl.when(j == 0)
+        def _():
+            send_in(1, 0)
+            send_in(1, 1)
+            send_rims(1)
+
+        return carry
+
+    lax.fori_loop(0, HEADS_HERE, sound, 0)
+    send_in(1, 2)
+    send_in(1, 3)
+
+    def video(j, carry):
+        for a in range(2):
+            from_sides(lambda d, a=a: rim_copy(j, a, d).wait_recv())
+            came_in(j, a)
+        for c in (0, 1, 2, 3, 6, 7):
+            turn(j, c)
+        came_in(j, 2)
+        came_in(j, 3)
+
+        def step(k, c):
             i = lax.rem(x + k, 4)
             part = pl.ds(pl.multiple_of(i * CHUNK, CHUNK), CHUNK)
             o, dq = attend(j, video_chunks, queries[j, part, :], grads[j, part, :])
             video_out[0, j, part, :] = o
             video_out[1, j, part, :] = dq
-            for a in range(2):
-                out_copy(j, a, 2 * k + 1, True).start()
-
-                @pl.when(k == 0)
-                def _(a=a):
-                    out_local(j, a).start()
-
-                @pl.when(k > 0)
-                def _(a=a):
-                    out_copy(j, a, 2 * k, True).start()
-
             return c
 
-        lax.fori_loop(0, 4, video_step, 0)
+        lax.fori_loop(0, 4, step, 0)
         for d in range(2):
             at = (BEFORE, AFTER)[d]
-            rim_grad_out[d, j, 0] = key_sum[at : at + CHUNK, :].astype(BF16)
-            rim_grad_out[d, j, 1] = value_sum[at : at + CHUNK, :].astype(BF16)
-        on_sides(lambda d: rim_grad_copy(j, d).start())
-        from_sides(lambda d: pool_grad_copy(j, d).wait_recv())
-        for a, summed in enumerate((key_sum, value_sum)):
-            pooled = summed[SHARED + POOLED : SHARED + 2 * POOLED, :]
-            for d in range(2):
-                pooled = pooled + pool_grad_in[d, j, a].astype(F32)
-            pooled = pooled * (POOL**-0.5)
-            spread = jnp.broadcast_to(pooled[:, None, :], (POOLED, POOL, HEAD))
-            whole = summed[:VIDEO, :] + spread.reshape(VIDEO, HEAD)
-            video_out[2 + a, j] = whole.astype(BF16)
-            out_local(j, 2 + a).start()
-
-            def across(i, c, a=a):
-                out_copy(j, 2 + a, 2 * i + 1, True).start()
-                return c
-
-            def along(i, c, a=a):
-                out_copy(j, 2 + a, 2 * i, True).start()
-                return c
-
-            lax.fori_loop(0, 4, across, 0)
-            lax.fori_loop(1, 4, along, 0)
-            sound_sum[j, a] = summed[OWN:BEFORE, :]
+            rim_grad_out[d, j, 0] = key_sum[j, at : at + CHUNK, :].astype(BF16)
+            rim_grad_out[d, j, 1] = value_sum[j, at : at + CHUNK, :].astype(BF16)
+        for i in range(8):
+            on_sides(lambda d, i=i: rim_grad_copy(j, d, i).start())
+        send_out(j, 0)
+        send_out(j, 1)
+        finish(j)
         return carry
 
-    lax.fori_loop(0, HEADS_HERE, head, 0)
-
-    prev_weight = blocks[jnp.maximum(tm - 1, 0), 1].astype(F32)
-    next_weight = blocks[jnp.minimum(tm + 1, lax.axis_size("tm") - 1), 0].astype(F32)
+    lax.fori_loop(0, HEADS_HERE, video, 0)
+
+    prev_weight = blocks[1, jnp.maximum(tm - 1, 0)].astype(F32)
+    next_weight = blocks[0, jnp.minimum(tm + 1, lax.axis_size("tm") - 1)].astype(F32)
     weights = (next_weight, prev_weight)
     for j in range(HEADS_HERE):
-        from_sides(lambda d, j=j: rim_grad_copy(j, d).wait_recv())
+        for i in range(8):
+            from_sides(lambda d, j=j, i=i: rim_grad_copy(j, d, i).wait_recv())
         for a in range(2):
             for b in range(2):
                 part = slice(b * CHUNK, (b + 1) * CHUNK)
-                whole = sound_sum[j, a, part, :]
+                whole = (key_sum, value_sum)[a][j, OWN + b * CHUNK : OWN + (b + 1) * CHUNK, :]
                 for d in range(2):
                     weight = weights[d] if b else 1.0 - weights[d]
                     whole = whole + rim_grad_in[d, j, a].astype(F32) * weight
@@ -454,25 +498,41 @@
         for a in range(4):
             sound_out(j, a).wait()
             out_local(j, a).wait()
-            lax.fori_loop(1, 8, lambda r, c, j=j, a=a: (out_copy(j, a, r, True).wait_send(), c)[1], 0)
-            lax.fori_loop(1, 8, lambda r, c, j=j, a=a: (out_copy(j, a, r, False).wait_recv(), c)[1], 0)
+            to_peers(lambda r, j=j, a=a: out_copy(j, a, r, True).wait_send())
+            to_peers(lambda r, j=j, a=a: out_copy(j, a, r, False).wait_recv())
         for a in range(2):
             on_sides(lambda d, j=j, a=a: rim_copy(j, a, d).wait_send())
             on_sides(lambda d, j=j, a=a: pooled_copy(j, a, d).wait_send())
         on_sides(lambda d, j=j: pool_grad_copy(j, d).wait_send())
-        on_sides(lambda d, j=j: rim_grad_copy(j, d).wait_send())
-    for a in range(4):
-        lax.fori_loop(1, 8, lambda r, c, a=a: (in_copy(1, a, r, True).wait_send(), c)[1], 0)
+        for i in range(8):
+            on_sides(lambda d, j=j, i=i: rim_grad_copy(j, d, i).wait_send())
+    for j in range(HEADS_HERE):
+        for a in range(4):
+            sent_in(j, a)
+    to_peers(lambda r: pool_copy(r).wait_send())
+
+
+def publish(*refs):
+    made, final, held, sem = refs[:8], refs[8:16], refs[16:24], refs[24]
+    reads = [pltpu.make_async_copy(made[i], held[i], sem.at[i]) for i in range(8)]
+    writes = [pltpu.make_async_copy(held[i], final[i], sem.at[8 + i]) for i in range(8)]
+    for read in reads:
+        read.start()
+    for read, write in zip(reads, writes):
+        read.wait()
+        write.start()
+    for write in writes:
+        write.wait()
 
 
 def per_device(*args):
     video = jax.ShapeDtypeStruct(args[0].shape, BF16)
     audio = jax.ShapeDtypeStruct(args[4].shape, BF16)
     two = HEADS_HERE
-    return pl.pallas_call(
+    made = pl.pallas_call(
         kernel,
         out_shape=(video,) * 4 + (audio,) * 4,
-        in_specs=[pl.BlockSpec(memory_space=pl.ANY)] * 8
+        in_specs=[pl.BlockSpec(memory_space=pltpu.HBM)] * 8
         + [pl.BlockSpec(memory_space=pltpu.SMEM)] * 2,
         out_specs=(pl.BlockSpec(memory_space=pl.ANY),) * 8,
         scratch_shapes=[
@@ -482,13 +542,16 @@
             pltpu.VMEM((two, VIDEO, HEAD), BF16),
             pltpu.VMEM((two, AUDIO, HEAD), BF16),
             pltpu.VMEM((two, AUDIO, HEAD), BF16),
-            pltpu.VMEM((HEAD, LISTED), BF16),
-            pltpu.VMEM((HEAD, LISTED), BF16),
-            pltpu.VMEM((LISTED, HEAD), F32),
-            pltpu.VMEM((LISTED, HEAD), F32),
+            pltpu.VMEM((two, HEAD, LISTED), BF16),
+            pltpu.VMEM((two, HEAD, LISTED), BF16),
+            pltpu.VMEM((two, LISTED, HEAD), F32),
+            pltpu.VMEM((two, LISTED, HEAD), F32),
             pltpu.VMEM((SHARED, CHUNK), F32),
             pltpu.VMEM((SHARED, CHUNK), BF16),
-            pltpu.VMEM((POOLED, VIDEO), BF16),
+            pltpu.VMEM((HEAD, 8 * two * HEAD), BF16),
+            pltpu.VMEM((HEAD, 8 * two * HEAD), BF16),
+            pltpu.VMEM((8, two, POOL, HEAD), BF16),
+            pltpu.VMEM((8, two, POOL, HEAD), BF16),
             pltpu.VMEM((4, two, VIDEO, HEAD), BF16),
             pltpu.VMEM((4, two, AUDIO, HEAD), BF16),
             pltpu.VMEM((2, 2, two, CHUNK, HEAD), BF16),
@@ -496,23 +559,35 @@
             pltpu.VMEM((2, two, 2, CHUNK, HEAD), BF16),
             pltpu.VMEM((2, two, 2, POOLED, HEAD), BF16),
             pltpu.VMEM((2, two, 2, POOLED, HEAD), BF16),
-            pltpu.VMEM((two, 2, AUDIO, HEAD), F32),
             pltpu.SemaphoreType.DMA((64,)),
             pltpu.SemaphoreType.DMA((64,)),
             pltpu.SemaphoreType.DMA((64,)),
             pltpu.SemaphoreType.DMA((64,)),
-            pltpu.SemaphoreType.DMA((24,)),
-            pltpu.SemaphoreType.DMA((24,)),
+            pltpu.SemaphoreType.DMA((52,)),
+            pltpu.SemaphoreType.DMA((52,)),
+            pltpu.SemaphoreType.DMA((8,)),
+            pltpu.SemaphoreType.DMA((8,)),
+            pltpu.SemaphoreType.DMA((2,)),
             pltpu.SemaphoreType.DMA((8,)),
             pltpu.SemaphoreType.DMA((8,)),
             pltpu.SemaphoreType.DMA((8,)),
             pltpu.SemaphoreType.DMA((8,)),
         ],
         compiler_params=pltpu.CompilerParams(
-            collective_id=0, has_side_effects=True, vmem_limit_bytes=48 * 1024 * 1024
+            collective_id=0, has_side_effects=True, vmem_limit_bytes=60 * 1024 * 1024
         ),
         name="joint_attention",
-    )(*args)
+    )(*args[:8], args[8].T, args[9].T)
+    return pl.pallas_call(
+        publish,
+        out_shape=(video,) * 4 + (audio,) * 4,
+        in_specs=[pl.BlockSpec(memory_space=pl.ANY)] * 8,
+        out_specs=(pl.BlockSpec(memory_space=pltpu.HBM),) * 8,
+        scratch_shapes=[pltpu.VMEM(args[0].shape, BF16)] * 4
+        + [pltpu.VMEM(args[4].shape, BF16)] * 4
+        + [pltpu.SemaphoreType.DMA((16,))],
+        name="publish",
+    )(*made)
 
 
 def solution(mesh):

time: 140 us -> 118 us (0.84)
  local copies, waits for them, and re-layouts: 13.8 us -> 0 us
  Pallas kernels: 124 us -> 117 us
    unnamed x26 -> x0, local copies, waits for them, and re-layouts: 13.8 us -> none
    pallas_call x1, Pallas kernels: 124 us -> 114 us  [per_device(): pl.pallas_call(kernel, out_shape=(video,) * 4 + (audio,) * 4, in_specs=[p...]
    pallas_call x0 -> x1, Pallas kernels: none -> 2.84 us  [per_device(): pl.pallas_call(publish, out_shape=(video,) * 4 + (audio,) * 4, in_specs=[...]
where the time goes in v2:
time: 118 us; the launch traced here: 117 us
  Pallas kernels  117 us (99%)
    pallas_call x1, Pallas kernels, per_device(): pl.pallas_call(kernel, out_shape=(video,) * 4 + (audio,) * 4, in_specs=[p...  114 us
    pallas_call x1, Pallas kernels, per_device(): pl.pallas_call(publish, out_shape=(video,) * 4 + (audio,) * 4, in_specs=[...  2.84 us

profile of v2, /device:TPU:34, one launch (start us, length us, event | category | flops | bytes accessed | tf_op | source)
XLA Modules:
  0.0 117.4 jit_solution(4248398030365196167)
XLA Ops:
  0.6 113.9 %joint_attention.1 = (bf16[128,2048]{1,0:T(8,128)(2,1)}, bf16[128,2048]{1,0:T(8,128)(2,1)}, bf16[128,2048]{1,0:T(8,128)(2,1)}, bf16[128,2048]{1,0:T(8,128)(2,1)}...) custom-call(bf16[128,2048]{1,0:T(8,128)(2,1)} %video_q.1, ...), custom_call_target="tpu_custom_call" | custom-call | tf_op jit(solution)/shard_map/joint_attention/pallas_call | solution.py:532
  114.5 2.8 %publish.1 = (bf16[128,2048]{1,0:T(8,128)(2,1)}, bf16[128,2048]{1,0:T(8,128)(2,1)}, bf16[128,2048]{1,0:T(8,128)(2,1)}, bf16[128,2048]{1,0:T(8,128)(2,1)}, bf16[5...) custom-call(bf16[128,2048]{1,0:T(8,128)(2,1)} %get-tuple-element.16.refs_0_,, ...), custom_call_target="tpu_custom_call" | custom-call | tf_op jit(solution)/shard_map/publish/pallas_call | solution.py:581

commit v3 on v2

--- a/solution.py
+++ b/solution.py
@@ -9,6 +9,7 @@
 CHUNK = 256
 POOL = 16
 HEADS_HERE = 2
+RUN = 8
 VIDEO = 1024
 AUDIO = 512
 POOLED = 64
@@ -66,6 +67,7 @@
     video_out,
     audio_out,
     rim_out,
+    relay_in,
     rim_grad_out,
     rim_grad_in,
     pool_grad_out,
@@ -78,6 +80,8 @@
     near_recv,
     pool_send,
     pool_recv,
+    relay_recv,
+    onward_send,
     local_rows,
     local_in,
     local_sound,
@@ -89,6 +93,12 @@
     x, half = lax.div(me, 2), lax.rem(me, 2)
     has_prev, has_next = tm > 0, tm < lax.axis_size("tm") - 1
     sides = ((has_prev, tm - 1), (has_next, tm + 1))
+    place_in_run = lax.rem(tm, RUN)
+    run_ends = (place_in_run == 0, place_in_run == RUN - 1)
+    at_end = run_ends[0] | run_ends[1]
+    other_end = jnp.where(run_ends[0], tm + RUN - 1, tm - RUN + 1)
+    run_below, run_above = tm >= RUN, tm < lax.axis_size("tm") - RUN
+    onward = ((run_ends[1] & run_below, tm - RUN), (run_ends[0] & run_above, tm + RUN))
 
     def target(r):
         return lax.rem(x + lax.div(r, 2), 4) * 2 + lax.rem(half + lax.rem(r, 2), 2)
@@ -203,6 +213,26 @@
             sides[d][1],
         )
 
+    def relay_copy(j, a, d):
+        return pltpu.make_async_remote_copy(
+            src_ref=rim_out.at[d, a, j],
+            dst_ref=relay_in.at[j, a],
+            send_sem=near_send.at[(j * 2 + a) * 2 + d],
+            recv_sem=relay_recv.at[j * 2 + a],
+            device_id=(other_end, me),
+            device_id_type=MESH,
+        )
+
+    def onward_copy(j, a, d):
+        return pltpu.make_async_remote_copy(
+            src_ref=relay_in.at[j, a],
+            dst_ref=(keys, values)[a].at[j, pl.ds((AFTER, BEFORE)[d], CHUNK), :],
+            send_sem=onward_send.at[j * 2 + a],
+            recv_sem=near_recv.at[(j * 2 + a) * 2 + d],
+            device_id=(onward[d][1], me),
+            device_id_type=MESH,
+        )
+
     def pooled_copy(j, a, d):
         listed = (keys, values)[a]
         return near_copy(
@@ -252,6 +282,16 @@
             barrier, inc=1, device_id=(sides[d][1], me), device_id_type=MESH
         )
     )
+    for there, device in (
+        (at_end, other_end),
+        (at_end & run_below, tm - RUN),
+        (at_end & run_above, tm + RUN),
+    ):
+
+        @pl.when(there)
+        def _(device=device):
+            pl.semaphore_signal(barrier, inc=1, device_id=(device, me), device_id_type=MESH)
+
     for a in range(2):
         rows_local(a).start()
     for j in range(HEADS_HERE):
@@ -306,7 +346,10 @@
             both = dot(upper, rows_k[:, part]) + dot(lower, rows_v[:, part])
             pool_stage[s, j] = (both * (POOL**-0.5)).astype(BF16)
 
-    pl.semaphore_wait(barrier, 7 + has_prev.astype(jnp.int32) + has_next.astype(jnp.int32))
+    one = jnp.int32(1)
+    greeted = 7 + jnp.where(has_prev, one, 0) + jnp.where(has_next, one, 0)
+    ends = one + jnp.where(run_below, one, 0) + jnp.where(run_above, one, 0)
+    pl.semaphore_wait(barrier, greeted + jnp.where(at_end, ends, 0))
 
     def to_peers(act):
         lax.fori_loop(0, 4, lambda i, c: (act(2 * i + 1), c)[1], 0)
@@ -327,13 +370,34 @@
         to_peers(lambda r: out_copy(j, a, r, True).start())
 
     def send_rims(j):
+        def start(a, d):
+            @pl.when(run_ends[d])
+            def _():
+                relay_copy(j, a, d).start()
+
+            @pl.when(jnp.logical_not(run_ends[d]))
+            def _():
+                rim_copy(j, a, d).start()
+
         for a in range(2):
-            on_sides(lambda d, a=a: rim_copy(j, a, d).start())
-
+            on_sides(lambda d, a=a: start(a, d))
+
+    def pass_on(j):
+        for d in range(2):
+
+            @pl.when(onward[d][0])
+            def _(d=d):
+                for a in range(2):
+                    relay_copy(j, a, d).wait_recv()
+                    onward_copy(j, a, d).start()
+
+    send_rims(0)
+    send_rims(1)
     to_peers(lambda r: pool_copy(r).start())
     send_in(0, 0)
+    pass_on(0)
     send_in(0, 1)
-    send_rims(0)
+    pass_on(1)
     pool_land[me] = pool_stage[me]
     to_peers(lambda r: pool_copy(r).wait_recv())
     for j in range(HEADS_HERE):
@@ -439,7 +503,6 @@
         def _():
             send_in(1, 0)
             send_in(1, 1)
-            send_rims(1)
 
         return carry
 
@@ -462,6 +525,17 @@
             o, dq = attend(j, video_chunks, queries[j, part, :], grads[j, part, :])
             video_out[0, j, part, :] = o
             video_out[1, j, part, :] = dq
+            for a in range(2):
+                out_copy(j, a, 2 * k + 1, True).start()
+
+                @pl.when(k == 0)
+                def _(a=a):
+                    out_local(j, a).start()
+
+                @pl.when(k > 0)
+                def _(a=a):
+                    out_copy(j, a, 2 * k, True).start()
+
             return c
 
         lax.fori_loop(0, 4, step, 0)
@@ -471,8 +545,6 @@
             rim_grad_out[d, j, 1] = value_sum[j, at : at + CHUNK, :].astype(BF16)
         for i in range(8):
             on_sides(lambda d, i=i: rim_grad_copy(j, d, i).start())
-        send_out(j, 0)
-        send_out(j, 1)
         finish(j)
         return carry
 
@@ -510,19 +582,22 @@
         for a in range(4):
             sent_in(j, a)
     to_peers(lambda r: pool_copy(r).wait_send())
+    for d in range(2):
+
+        @pl.when(onward[d][0])
+        def _(d=d):
+            for j in range(HEADS_HERE):
+                for a in range(2):
+                    onward_copy(j, a, d).wait_send()
 
 
 def publish(*refs):
-    made, final, held, sem = refs[:8], refs[8:16], refs[16:24], refs[24]
-    reads = [pltpu.make_async_copy(made[i], held[i], sem.at[i]) for i in range(8)]
-    writes = [pltpu.make_async_copy(held[i], final[i], sem.at[8 + i]) for i in range(8)]
-    for read in reads:
-        read.start()
-    for read, write in zip(reads, writes):
-        read.wait()
-        write.start()
-    for write in writes:
-        write.wait()
+    sem = refs[16]
+    copies = [pltpu.make_async_copy(refs[i], refs[8 + i], sem.at[i]) for i in range(8)]
+    for copy in copies:
+        copy.start()
+    for copy in copies:
+        copy.wait()
 
 
 def per_device(*args):
@@ -531,10 +606,10 @@
     two = HEADS_HERE
     made = pl.pallas_call(
         kernel,
-        out_shape=(video,) * 4 + (audio,) * 4,
+        out_shape=(pltpu.VMEM(video.shape, BF16),) * 4 + (pltpu.VMEM(audio.shape, BF16),) * 4,
         in_specs=[pl.BlockSpec(memory_space=pltpu.HBM)] * 8
         + [pl.BlockSpec(memory_space=pltpu.SMEM)] * 2,
-        out_specs=(pl.BlockSpec(memory_space=pl.ANY),) * 8,
+        out_specs=(pl.BlockSpec(memory_space=pltpu.VMEM),) * 8,
         scratch_shapes=[
             pltpu.VMEM((two, LISTED, HEAD), BF16),
             pltpu.VMEM((two, LISTED, HEAD), BF16),
@@ -555,6 +630,7 @@
             pltpu.VMEM((4, two, VIDEO, HEAD), BF16),
             pltpu.VMEM((4, two, AUDIO, HEAD), BF16),
             pltpu.VMEM((2, 2, two, CHUNK, HEAD), BF16),
+            pltpu.VMEM((two, 2, CHUNK, HEAD), BF16),
             pltpu.VMEM((2, two, 2, CHUNK, HEAD), BF16),
             pltpu.VMEM((2, two, 2, CHUNK, HEAD), BF16),
             pltpu.VMEM((2, two, 2, POOLED, HEAD), BF16),
@@ -567,6 +643,8 @@
             pltpu.SemaphoreType.DMA((52,)),
             pltpu.SemaphoreType.DMA((8,)),
             pltpu.SemaphoreType.DMA((8,)),
+            pltpu.SemaphoreType.DMA((4,)),
+            pltpu.SemaphoreType.DMA((4,)),
             pltpu.SemaphoreType.DMA((2,)),
             pltpu.SemaphoreType.DMA((8,)),
             pltpu.SemaphoreType.DMA((8,)),
@@ -583,9 +661,8 @@
         out_shape=(video,) * 4 + (audio,) * 4,
         in_specs=[pl.BlockSpec(memory_space=pl.ANY)] * 8,
         out_specs=(pl.BlockSpec(memory_space=pltpu.HBM),) * 8,
-        scratch_shapes=[pltpu.VMEM(args[0].shape, BF16)] * 4
-        + [pltpu.VMEM(args[4].shape, BF16)] * 4
-        + [pltpu.SemaphoreType.DMA((16,))],
+        scratch_shapes=[pltpu.SemaphoreType.DMA((8,))],
+        compiler_params=pltpu.CompilerParams(vmem_limit_bytes=1024 * 1024),
         name="publish",
     )(*made)
 

time: 118 us -> 116 us (0.983); the launches traced: 117 us -> 114 us
  Pallas kernels: 117 us -> 113 us
    pallas_call x1, Pallas kernels: 114 us -> 111 us  [per_device(): pl.pallas_call(kernel, out_shape=(pltpu.VMEM(video.shape, BF16),) * 4 + (...]
where the time goes in v3:
time: 116 us; the launch traced here: 114 us
  Pallas kernels  113 us (97%)
    pallas_call x1, Pallas kernels, per_device(): pl.pallas_call(kernel, out_shape=(pltpu.VMEM(video.shape, BF16),) * 4 + (...  111 us

profile of v3, /device:TPU:34, one launch (start us, length us, event | category | flops | bytes accessed | tf_op | source)
XLA Modules:
  0.0 113.6 jit_solution(4930004911022841695)
XLA Ops:
  0.6 111.2 %joint_attention.1 = (bf16[128,2048]{1,0:T(8,128)(2,1)S(1)}, bf16[128,2048]{1,0:T(8,128)(2,1)S(1)}, bf16[128,2048]{1,0:T(8,128)(2,1)S(1)}, bf16[128,2048]{1,0:T(...) custom-call(bf16[128,2048]{1,0:T(8,128)(2,1)} %video_q.1, ...), custom_call_target="tpu_custom_call" | custom-call | tf_op jit(solution)/shard_map/joint_attention/pallas_call | solution.py:607
  111.8 1.7 %publish.1 = (bf16[128,2048]{1,0:T(8,128)(2,1)}, bf16[128,2048]{1,0:T(8,128)(2,1)}, bf16[128,2048]{1,0:T(8,128)(2,1)}, bf16[128,2048]{1,0:T(8,128)(2,1)}, bf16[5...) custom-call(bf16[128,2048]{1,0:T(8,128)(2,1)S(1)} %get-tuple-element.16.refs, ...), custom_call_target="tpu_custom_call" | custom-call | tf_op jit(solution)/shard_map/publish/pallas_call | solution.py:659

commit v4 on v3

--- a/solution.py
+++ b/solution.py
@@ -352,8 +352,7 @@
     pl.semaphore_wait(barrier, greeted + jnp.where(at_end, ends, 0))
 
     def to_peers(act):
-        lax.fori_loop(0, 4, lambda i, c: (act(2 * i + 1), c)[1], 0)
-        lax.fori_loop(1, 4, lambda i, c: (act(2 * i), c)[1], 0)
+        lax.fori_loop(1, 8, lambda r, c: (act(r), c)[1], 0)
 
     def send_in(j, a):
         to_peers(lambda r: in_copy(j, a, r, True).start())

time: 116 us -> 115 us (level)
  no operation moved by 1% of the time
where the time goes in v4:
time: 115 us; the launch traced here: 114 us
  Pallas kernels  113 us (98%)
    pallas_call x1, Pallas kernels, per_device(): pl.pallas_call(kernel, out_shape=(pltpu.VMEM(video.shape, BF16),) * 4 + (...  111 us

profile of v4, /device:TPU:34, one launch (start us, length us, event | category | flops | bytes accessed | tf_op | source)
XLA Modules:
  0.0 113.5 jit_solution(15689194770732072262)
XLA Ops:
  0.6 111.2 %joint_attention.1 = (bf16[128,2048]{1,0:T(8,128)(2,1)S(1)}, bf16[128,2048]{1,0:T(8,128)(2,1)S(1)}, bf16[128,2048]{1,0:T(8,128)(2,1)S(1)}, bf16[128,2048]{1,0:T(...) custom-call(bf16[128,2048]{1,0:T(8,128)(2,1)} %video_q.1, ...), custom_call_target="tpu_custom_call" | custom-call | tf_op jit(solution)/shard_map/joint_attention/pallas_call | solution.py:606
  111.8 1.7 %publish.1 = (bf16[128,2048]{1,0:T(8,128)(2,1)}, bf16[128,2048]{1,0:T(8,128)(2,1)}, bf16[128,2048]{1,0:T(8,128)(2,1)}, bf16[128,2048]{1,0:T(8,128)(2,1)}, bf16[5...) custom-call(bf16[128,2048]{1,0:T(8,128)(2,1)S(1)} %get-tuple-element.16.refs, ...), custom_call_target="tpu_custom_call" | custom-call | tf_op jit(solution)/shard_map/publish/pallas_call | solution.py:658
